TPU v7x, 128 devices: a whole 4x4x4 slice. The times are simulated.
128 devices in a mesh: dp: 4 (over y), ctx: 32 (over z, x, core).
Axes of the slice: x: 4, y: 4, z: 4, core: 2. Of those that a mesh axis runs over, the one named last changes fastest.
Arguments:
- tokens: bfloat16 [4, 4096, 2048], P('dp', 'ctx'), may hold values from -6 to 6
- queries: bfloat16 [4, 4096, 2048], P('dp', 'ctx'), may hold values from -6 to 6
- values: bfloat16 [4, 4096, 2048], P('dp', 'ctx'), may hold values from -6 to 6
- key_weight: bfloat16 [2048, 2048], replicated, may hold values from -0.125 to 0.125
- grad_out: bfloat16 [4, 4096, 2048], P('dp', 'ctx'), may hold values from -6 to 6
Outputs:
- attended: bfloat16 [4, 4096, 2048], P('dp', 'ctx')
- grad_tokens: bfloat16 [4, 4096, 2048], P('dp', 'ctx')
- grad_queries: bfloat16 [4, 4096, 2048], P('dp', 'ctx')
- grad_values: bfloat16 [4, 4096, 2048], P('dp', 'ctx')
- grad_key_weight: float32 [2048, 2048], P('ctx')
All inputs are finite; a program needn't handle non-finite values.
Results may differ from a plain program's by a relative error of at most 0.024.
Values may be sent and summed in bfloat16 or wider, within the bound.
A program may use at most 128 MiB of HBM per device.

v0:
```python
import math

import jax
import jax.numpy as jnp
import numpy as np
from jax import lax
from jax.experimental import pallas as pl
from jax.experimental.pallas import tpu as pltpu
from jax.sharding import PartitionSpec as P

DH = 128
TOK = 128
D = 2048
HALF = D // 2
GROUPS = 4
GC = HALF // GROUPS
SCALE = DH ** (-0.5)
BF = jnp.bfloat16
F32 = jnp.float32
MESH = pl.DeviceIdType.MESH
N_SEM = 160


def matrices():
    pool = np.zeros((224, 384), np.float32)
    for tok in range(256):
        pool[tok // 2, tok] = 0.5
        pool[128 + tok // 4, tok] = 0.25
        pool[192 + tok // 8, tok] = 0.125
    rise = np.zeros((96, 384), np.float32)
    for row in range(64):
        rise[row // 4, row] = 0.25
        rise[64 + row // 8, row] = 0.125
        rise[16 + row // 4, 128 + row] = 0.25
        rise[72 + row // 8, 128 + row] = 0.125
        rise[32 + row // 2, 192 + row] = 0.5
        rise[80 + row // 4, 192 + row] = 0.25
    third = np.zeros((64, 128), np.float32)
    for row in range(64):
        third[row, row] = 1.0
        third[row, 64 + row // 2] = 0.5
        third[row, 96 + row // 2] = 0.5
    back = np.zeros((128, 384), np.float32)
    for row in range(64):
        back[row, :128] = third[16 + row // 4] * 0.25
        back[64 + row, :128] = third[32 + row // 2] * 0.5
    spread = np.zeros((256, 384), np.float32)
    for tok in range(256):
        spread[tok, tok // 2] = 0.5
        spread[tok, 128 + tok // 4] = 0.25
        spread[tok, 192 + tok // 8] = 0.125
        spread[tok, 224 + tok // 8] = 0.125
        spread[tok, 256:384] = third[tok // 16] / 16
    return np.concatenate([pool, rise, back, spread], 0)


def flipped(place, k):
    if k == 0:
        return place
    if k == 1:
        return place + 1 - 2 * (place % 2)
    if k == 2:
        return place + 2 - 4 * (place // 2)
    return 3 - place


def nn(a, b):
    return lax.dot_general(a, b, (((1,), (0,)), ((), ())), preferred_element_type=F32)


def nt(a, b):
    return lax.dot_general(a, b, (((1,), (1,)), ((), ())), preferred_element_type=F32)


def tn(a, b):
    return lax.dot_general(a, b, (((0,), (0,)), ((), ())), preferred_element_type=F32)


SCRATCH = dict(
    xa=((4 * 256, D), BF),
    wv=((GROUPS, D, GC), BF),
    qv=((256, HALF), BF),
    gv=((256, HALF), BF),
    kl=((2, 192, HALF), BF),
    vl=((2, 192, HALF), BF),
    cc=((2, 256, HALF), BF),
    sp=((2, 96, HALF), BF),
    sz=((2, 96, HALF), BF),
    dcb=((2, 256, HALF), BF),
    dcf=((2, 128, HALF), F32),
    rb=((2, 384, HALF), BF),
    sx=((2, 128, HALF), BF),
    ld=((2, 256, HALF), F32),
    gkv=((2, 256, HALF), BF),
    ao=((256, HALF), BF),
    qo=((256, HALF), BF),
    gy=((2, 4, 256, 128), BF),
    gt=((128, 1024), BF),
    rs=((2, 4, 4, 128, 128), BF),
    ra=((2, 3, 4, 128, 128), BF),
    tf=((2, 4, 128, 128), F32),
    tb=((2, 4, 128, 128), BF),
    rz=((2, 3, 128, 128), BF),
    fo=((2, 128, 128), BF),
    ow=((64, D), BF),
    gxf=((128, D), F32),
    gxs=((128, D), BF),
    gxr=((128, D), BF),
    gxo=((128, D), BF),
    pp=((704, 384), BF),
)


def kernel(x_h, q_h, v_h, w_h, g_h, p_h, att_h, gx_h, gq_h, gvo_h, gw_h, *rest):
    s = dict(zip(SCRATCH, rest[: len(SCRATCH)]))
    ssem, rsem = rest[len(SCRATCH) :]
    xa, wv, qv, gv, kl, vl, cc = (s[n] for n in ("xa", "wv", "qv", "gv", "kl", "vl", "cc"))
    sp, sz, dcb, dcf, rb, sx, ld = (s[n] for n in ("sp", "sz", "dcb", "dcf", "rb", "sx", "ld"))
    gkv, ao, qo, gy, gt = (s[n] for n in ("gkv", "ao", "qo", "gy", "gt"))
    rs, ra, tf, tb, rz, fo, ow = (s[n] for n in ("rs", "ra", "tf", "tb", "rz", "fo", "ow"))
    gxf, gxs, gxr, gxo, pp = (s[n] for n in ("gxf", "gxs", "gxr", "gxo", "pp"))

    y = lax.axis_index("dp")
    ctx = lax.axis_index("ctx")
    core = ctx % 2
    xx = (ctx // 2) % 4
    zz = ctx // 8
    mate = (y, ctx + 1 - 2 * core)
    along_x = [(y, zz * 8 + flipped(xx, k) * 2 + core) for k in range(4)]
    along_z = [(y, flipped(zz, k) * 8 + xx * 2 + core) for k in range(4)]
    along_y = [(flipped(y, k), ctx) for k in range(4)]
    cross_y = [(flipped(y, k), mate[1]) for k in range(4)]
    mine = pl.multiple_of(core * HALF, HALF)
    theirs = pl.multiple_of((1 - core) * HALF, HALF)

    count = [0]
    sent = []
    stored = []

    def remote(src, dst, device):
        at = count[0]
        count[0] += 1
        copy = pltpu.make_async_remote_copy(
            src_ref=src, dst_ref=dst, send_sem=ssem.at[at], recv_sem=rsem.at[at], device_id=device, device_id_type=MESH
        )
        copy.start()
        sent.append(copy)
        return copy

    def local(src, dst):
        at = count[0]
        count[0] += 1
        copy = pltpu.make_async_copy(src, dst, ssem.at[at])
        copy.start()
        return copy

    def arrive(copies):
        for copy in copies:
            copy.wait_recv()

    def cols(j):
        return pl.ds(j * GC, GC)

    in_x = local(x_h, xa.at[0:128])
    in_v = local(v_h.at[:, pl.ds(mine, HALF)], vl.at[0, 0:128])
    in_p = local(p_h, pp)
    in_w = [local(w_h.at[:, pl.ds(pl.multiple_of(mine + j * GC, GC), GC)], wv.at[j]) for j in range(GROUPS)]
    in_q = local(q_h.at[:, pl.ds(mine, HALF)], qv.at[0:128])
    in_g = local(g_h.at[:, pl.ds(mine, HALF)], gv.at[0:128])

    peers = [mate] + along_x[1:] + along_z[1:] + along_y[1:] + cross_y[1:]
    barrier = pltpu.get_barrier_semaphore()
    for peer in peers:
        pl.semaphore_signal(barrier, inc=1, device_id=peer, device_id_type=MESH)
    pl.semaphore_wait(barrier, len(peers))

    m_v = remote(v_h.at[:, pl.ds(theirs, HALF)], vl.at[1, 0:128], mate)
    m_x = remote(x_h, xa.at[128:256], mate)
    m_q = remote(q_h.at[:, pl.ds(theirs, HALF)], qv.at[128:256], mate)
    m_g = remote(g_h.at[:, pl.ds(theirs, HALF)], gv.at[128:256], mate)
    y_x = [None] + [remote(x_h, xa.at[k * 256 : k * 256 + 128], along_y[k]) for k in (1, 2, 3)]

    def pooled(kv, ref, j, both):
        rows = nn(pp[0:224, 0:256], both).astype(BF)
        ref[1, 128:192, cols(j)] = rows[0:64]
        ref[0, 128:192, cols(j)] = rows[64:128]
        sp[kv, :, cols(j)] = rows[128:224]

    def send_x(kv, at):
        return [
            remote(sp.at[kv, 0:64, at], cc.at[kv, 0:64, at], along_x[1]),
            remote(sp.at[kv, 64:96, at], cc.at[kv, 64:96, at], along_x[2]),
            remote(sp.at[kv, 64:96, at], cc.at[kv, 96:128, at], along_x[3]),
        ]

    def rise(kv, j):
        rows = nn(pp[224:320, 0:64], sp[kv, 0:64, cols(j)]) + nn(pp[224:320, 128:256], cc[kv, 0:128, cols(j)])
        sz[kv, :, cols(j)] = rows.astype(BF)

    def send_z(kv, at):
        return [
            remote(sz.at[kv, 0:64, at], cc.at[kv, 128:192, at], along_z[1]),
            remote(sz.at[kv, 64:96, at], cc.at[kv, 192:224, at], along_z[2]),
            remote(sz.at[kv, 64:96, at], cc.at[kv, 224:256, at], along_z[3]),
        ]

    everything = pl.ds(0, HALF)

    in_p.wait()
    in_v.wait()
    m_v.wait_recv()
    for j in range(GROUPS):
        pooled(1, vl, j, jnp.concatenate([vl[0, 0:128, cols(j)], vl[1, 0:128, cols(j)]], 0))
    vx = send_x(1, everything)

    in_x.wait()
    m_x.wait_recv()
    kx = []
    for j in range(GROUPS):
        in_w[j].wait()
        keys = nn(xa[0:256, :], wv[j]).astype(BF)
        kl[0, 0:128, cols(j)] = keys[0:128]
        kl[1, 0:128, cols(j)] = keys[128:256]
        pooled(0, kl, j, keys)
        kx.append(send_x(0, cols(j)))

    arrive(vx)
    for j in range(GROUPS):
        rise(1, j)
    vz = send_z(1, everything)
    kz = []
    for j in range(GROUPS):
        arrive(kx[j])
        rise(0, j)
        kz.append(send_z(0, cols(j)))

    in_q.wait()
    in_g.wait()
    m_q.wait_recv()
    m_g.wait_recv()

    def head(at):
        c = pl.ds(at, DH)
        q = qv[:, c]
        g = gv[:, c]
        ck = cc[0, :, c]
        cv = cc[1, :, c]
        rate = SCALE * math.log2(math.e)
        e1 = jnp.exp2(nt(q, ck) * rate)
        total = jnp.sum(e1, -1, keepdims=True)
        pair = [slice(0, 128), slice(128, 256)]
        e0 = [jnp.exp2(nt(q[pair[b]], kl[b, :, c]) * rate) for b in (0, 1)]
        total = total + jnp.concatenate([jnp.sum(e, -1, keepdims=True) for e in e0], 0)
        inverse = 1.0 / (total * 0.25)
        p1 = e1 * inverse
        p0 = [e0[b] * inverse[pair[b]] for b in (0, 1)]
        p1b = p1.astype(BF)
        p0b = [p.astype(BF) for p in p0]
        out = (nn(p1b, cv) + jnp.concatenate([nn(p0b[b], vl[b, :, c]) for b in (0, 1)], 0)) * 0.25
        ao[:, c] = out.astype(BF)
        delta = jnp.sum(g.astype(F32) * out, -1, keepdims=True)
        d1 = (p1 * (nt(g, cv) - delta)).astype(BF)
        d0 = [(p0[b] * (nt(g[pair[b]], vl[b, :, c]) - delta[pair[b]])).astype(BF) for b in (0, 1)]
        fold = SCALE * 0.25
        dq = (nn(d1, ck) + jnp.concatenate([nn(d0[b], kl[b, :, c]) for b in (0, 1)], 0)) * fold
        qo[:, c] = dq.astype(BF)
        dck = tn(d1, q) * fold
        dcv = tn(p1b, g) * 0.25
        dcf[0, :, c] = dck[0:128]
        dcf[1, :, c] = dcv[0:128]
        dcb[0, 128:256, c] = dck[128:256].astype(BF)
        dcb[1, 128:256, c] = dcv[128:256].astype(BF)
        for b in (0, 1):
            dk = tn(d0[b], q[pair[b]]) * fold
            dv = tn(p0b[b], g[pair[b]]) * 0.25
            ld[0, pair[b], c] = dk[0:128]
            ld[1, pair[b], c] = dv[0:128]
            other = slice(64 - 64 * b, 128 - 64 * b)
            rb[0, other, c] = dk[128:192].astype(BF)
            rb[1, other, c] = dv[128:192].astype(BF)

    def attend(j):
        arrive(kz[j])

        def step(i, carry):
            head(pl.multiple_of(j * GC + i * DH, DH))
            return carry

        lax.fori_loop(0, GC // DH, step, 0)
        at = cols(j)
        return [
            remote(dcb.at[:, 128:192, at], rb.at[:, 256:320, at], along_z[1]),
            remote(dcb.at[:, 192:224, at], rb.at[:, 320:352, at], along_z[2]),
            remote(dcb.at[:, 224:256, at], rb.at[:, 352:384, at], along_z[3]),
        ]

    def return_x(j, copies):
        arrive(copies)
        at = cols(j)
        for kv in (0, 1):
            sx[kv, :, at] = (dcf[kv, :, at] + nn(pp[320:448, 0:128], rb[kv, 256:384, at])).astype(BF)
        return [
            remote(sx.at[:, 0:64, at], rb.at[:, 128:192, at], along_x[1]),
            remote(sx.at[:, 64:96, at], rb.at[:, 192:224, at], along_x[2]),
            remote(sx.at[:, 96:128, at], rb.at[:, 224:256, at], along_x[3]),
        ]

    def finish(j, copies):
        arrive(copies)
        at = cols(j)
        for kv in (0, 1):
            gkv[kv, :, at] = (ld[kv, :, at] + nn(pp[448:704, :], rb[kv, :, at])).astype(BF)

    def send_y(half):
        copies = []
        for k in (1, 2, 3):
            at = pl.ds(pl.multiple_of((half * 4 + flipped(y, k)) * DH, DH), DH)
            copies.append(remote(gkv.at[0, :, at], gy.at[half, k], along_y[k]))
        return copies

    def forward(k):
        y_x[k].wait_recv()
        return remote(xa.at[k * 256 : k * 256 + 128], xa.at[k * 256 + 128 : k * 256 + 256], mate)

    def weights(half, copies):
        own = pl.ds(pl.multiple_of((half * 4 + y) * DH, DH), DH)
        gt[:, 0:256] = gkv[0, :, own].T
        arrive(copies)
        for k in (1, 2, 3):
            gt[:, k * 256 : (k + 1) * 256] = gy[half, k].T

        def step(i, carry):
            part = nn(gt[...], xa[:, pl.ds(pl.multiple_of(i * 256, 256), 256)]).astype(BF)
            z_at = i // 2
            x_at = 2 * (i % 2)
            if half == 0:
                rs[0, x_at, z_at] = part[:, 0:128]
                rs[0, x_at + 1, z_at] = part[:, 128:256]
            else:
                rs[1, z_at, x_at] = part[:, 0:128]
                rs[1, z_at, x_at + 1] = part[:, 128:256]
            return carry

        lax.fori_loop(0, 8, step, 0)
        place, line = (xx, along_x) if half == 0 else (zz, along_z)
        return [remote(rs.at[half, flipped(place, k)], ra.at[half, k - 1], line[k]) for k in (1, 2, 3)]

    def second(half, copies):
        place = xx if half == 0 else zz
        arrive(copies)
        total = rs[half, place].astype(F32)
        for k in range(3):
            total = total + ra[half, k].astype(F32)
        tf[half] = total
        tb[half] = total.astype(BF)
        place, line = (zz, along_z) if half == 0 else (xx, along_x)
        return [remote(tb.at[half, flipped(place, k)], rz.at[half, k - 1], line[k]) for k in (1, 2, 3)]

    def third(half, copies):
        place = zz if half == 0 else xx
        arrive(copies)
        total = tf[half, place]
        for k in range(3):
            total = total + rz[half, k].astype(F32)
        fo[half] = total.T.astype(BF)
        at = pl.ds(pl.multiple_of((core * 8 + half * 4 + y) * DH, DH), DH)
        same = pl.ds(pl.multiple_of(core * 64, 64), 64)
        cross = pl.ds(pl.multiple_of(64 - core * 64, 64), 64)
        ow[:, at] = fo[half, same, :]
        return [remote(fo.at[half, same], ow.at[:, at], along_y[k]) for k in (1, 2, 3)] + [
            remote(fo.at[half, cross], ow.at[:, at], cross_y[k]) for k in range(4)
        ]

    def give(staged, out):
        stored.append(local(staged.at[0:128], out.at[:, pl.ds(mine, HALF)]))
        return remote(staged.at[128:256], out.at[:, pl.ds(mine, HALF)], mate)

    arrive(vz)
    bz0 = attend(0)
    bz1 = attend(1)
    bx0 = return_x(0, bz0)
    f1 = forward(1)
    bz2 = attend(2)
    bx1 = return_x(1, bz1)
    f3 = forward(3)
    finish(0, bx0)
    bz3 = attend(3)
    given = [give(ao, att_h), give(qo, gq_h)]
    bx2 = return_x(2, bz2)
    finish(1, bx1)
    gy0 = send_y(0)
    f2 = forward(2)
    bx3 = return_x(3, bz3)
    finish(2, bx2)
    arrive([f1, f2, f3])
    ax0 = weights(0, gy0)
    finish(3, bx3)
    gy1 = send_y(1)
    given.append(give(gkv.at[1], gvo_h))
    bx0 = second(0, ax0)
    ax1 = weights(1, gy1)

    def partial(i, carry):
        at = pl.ds(pl.multiple_of(i * 256, 256), 256)
        total = nt(gkv[0, :, cols(0)], wv[0, at, :])
        for j in range(1, GROUPS):
            total = total + nt(gkv[0, :, cols(j)], wv[j, at, :])
        gxf[:, at] = total[0:128]
        gxs[:, at] = total[128:256].astype(BF)
        return carry

    lax.fori_loop(0, 8, partial, 0)
    gxc = remote(gxs, gxr, mate)
    last0 = third(0, bx0)
    bx1 = second(1, ax1)
    gxc.wait_recv()
    gxo[...] = (gxf[...] + gxr[...].astype(F32)).astype(BF)
    stored.append(local(gxo, gx_h))
    last1 = third(1, bx1)
    arrive(last0)
    arrive(last1)
    stored.append(local(ow, gw_h))
    arrive(given)
    for copy in stored:
        copy.wait()
    for copy in sent:
        copy.wait_send()


def body(tokens, queries, values, key_weight, grad_out):
    anywhere = pl.BlockSpec(memory_space=pl.ANY)
    block = jax.ShapeDtypeStruct((TOK, D), BF)
    att, gx, gq, gv, gw = pl.pallas_call(
        kernel,
        out_shape=[block] * 4 + [jax.ShapeDtypeStruct((64, D), BF)],
        in_specs=[anywhere] * 6,
        out_specs=[anywhere] * 5,
        scratch_shapes=[pltpu.VMEM(shape, dtype) for shape, dtype in SCRATCH.values()]
        + [pltpu.SemaphoreType.DMA((N_SEM,)), pltpu.SemaphoreType.DMA((N_SEM,))],
        compiler_params=pltpu.CompilerParams(
            collective_id=0, has_side_effects=True, vmem_limit_bytes=56 * 1024 * 1024
        ),
        name="hierarchical_attention",
    )(tokens[0], queries[0], values[0], key_weight, grad_out[0], jnp.asarray(matrices(), BF))
    return att[None], gx[None], gq[None], gv[None], gw.astype(F32)


def solution(mesh):
    split = P("dp", "ctx", None)
    return jax.shard_map(
        body,
        mesh=mesh,
        in_specs=(split, split, split, P(), split),
        out_specs=(split, split, split, split, P("ctx", None)),
        check_vma=False,
    )
```

profile of v0, /device:TPU:1, one launch (start us, length us, event | category | flops | bytes accessed | tf_op | source)
XLA Modules:
  0.0 83.9 jit_solution(12026713407405241372)
XLA Ops:
  0.6 74.0 %hierarchical_attention.1 = (bf16[128,2048]{1,0:T(8,128)(2,1)}, bf16[128,2048]{1,0:T(8,128)(2,1)}, bf16[128,2048]{1,0:T(8,128)(2,1)}, bf16[128,2048]{1,0:T(8,128)(2,1)}, bf16[64,2048]{1,0:T(8,128)(2,1)}) custom-call(bf16[128,2048]{1,0:T(8,128)(2,1)} %bitcast.12, bf16[128,2048]{1,0:T(8,128)(2,1)} %bitcast.13, bf16[128,2048]{1,0:T(8,128)(2,1)} %bitcast.14, ...), custom_call_target="tpu_custom_call" | custom-call | tf_op jit(solution)/shard_map/hierarchical_attention/pallas_call | solution.py:433
  74.6 1.8 %convert_element_type.3 = f32[64,2048]{1,0:T(8,128)} convert(bf16[64,2048]{1,0:T(8,128)(2,1)} %get-tuple-element.14) | non-fusion elementwise | flops 131072 | bytes 786432 | tf_op jit(solution)/shard_map/convert_element_type | solution.py:445
  76.4 1.9 %copy.15 = bf16[1,128,2048]{2,1,0:T(8,128)(2,1)} copy(bf16[1,128,2048]{2,1,0:T(8,128)(2,1)} %bitcast.11) | data formatting | bytes 1048576
  78.3 1.9 %copy.16 = bf16[1,128,2048]{2,1,0:T(8,128)(2,1)} copy(bf16[1,128,2048]{2,1,0:T(8,128)(2,1)} %bitcast.10) | data formatting | bytes 1048576
  80.1 1.9 %copy.17 = bf16[1,128,2048]{2,1,0:T(8,128)(2,1)} copy(bf16[1,128,2048]{2,1,0:T(8,128)(2,1)} %bitcast.9) | data formatting | bytes 1048576
  82.0 1.9 %copy.18 = bf16[1,128,2048]{2,1,0:T(8,128)(2,1)} copy(bf16[1,128,2048]{2,1,0:T(8,128)(2,1)} %bitcast.8) | data formatting | bytes 1048576
where the time goes:
time: 84.2 us; the launch traced here: 83.9 us
  Pallas kernels  74 us (88%)
  local copies, waits for them, and re-layouts  7.52 us (9%)
  other arithmetic  1.78 us (2%)
    pallas_call x1, Pallas kernels, body(): pl.pallas_call(kernel, out_shape=[block] * 4 + [jax.ShapeDtypeStruct((64,...  74 us
    unnamed x4, local copies, waits for them, and re-layouts  7.52 us
    convert_element_type x1, other arithmetic, body(): return (att[None], gx[None], gq[None], gv[None], gw.astype(F32))  1.78 us

commit v1 on v0

v1 whole, which is shorter than its diff:
```python
import math

import jax
import jax.numpy as jnp
import numpy as np
from jax import lax
from jax.experimental import pallas as pl
from jax.experimental.pallas import tpu as pltpu
from jax.sharding import PartitionSpec as P

DH = 128
TOK = 128
D = 2048
HALF = D // 2
GROUPS = 4
GC = HALF // GROUPS
SCALE = DH ** (-0.5)
BF = jnp.bfloat16
F32 = jnp.float32
MESH = pl.DeviceIdType.MESH
N_SEM = 208


def matrices():
    pool = np.zeros((112, 384), np.float32)
    for tok in range(128):
        pool[tok // 2, tok] = 0.5
        pool[64 + tok // 4, tok] = 0.25
        pool[96 + tok // 8, tok] = 0.125
    rise = np.zeros((96, 384), np.float32)
    for row in range(64):
        rise[row // 4, row] = 0.25
        rise[64 + row // 8, row] = 0.125
        rise[16 + row // 4, 128 + row] = 0.25
        rise[72 + row // 8, 128 + row] = 0.125
        rise[32 + row // 2, 192 + row] = 0.5
        rise[80 + row // 4, 192 + row] = 0.25
    third = np.zeros((64, 128), np.float32)
    for row in range(64):
        third[row, row] = 1.0
        third[row, 64 + row // 2] = 0.5
        third[row, 96 + row // 2] = 0.5
    back = np.zeros((128, 384), np.float32)
    for row in range(64):
        back[row, :128] = third[16 + row // 4] * 0.25
        back[64 + row, :128] = third[32 + row // 2] * 0.5
    spread = np.zeros((256, 384), np.float32)
    for tok in range(256):
        spread[tok, tok // 2] = 0.5
        spread[tok, 128 + tok // 4] = 0.25
        spread[tok, 192 + tok // 8] = 0.125
        spread[tok, 224 + tok // 8] = 0.125
        spread[tok, 256:384] = third[tok // 16] / 16
    return np.concatenate([pool, rise, back, spread], 0)


def flipped(place, k):
    if k == 0:
        return place
    if k == 1:
        return place + 1 - 2 * (place % 2)
    if k == 2:
        return place + 2 - 4 * (place // 2)
    return 3 - place


def nn(a, b):
    return lax.dot_general(a, b, (((1,), (0,)), ((), ())), preferred_element_type=F32)


def nt(a, b):
    return lax.dot_general(a, b, (((1,), (1,)), ((), ())), preferred_element_type=F32)


def tn(a, b):
    return lax.dot_general(a, b, (((0,), (0,)), ((), ())), preferred_element_type=F32)


SCRATCH = dict(
    xa=((4 * 256, D), BF),
    wv=((2, GROUPS, D, GC), BF),
    qv=((256, HALF), BF),
    gv=((256, HALF), BF),
    kl=((2, 192, HALF), BF),
    vl=((2, 192, HALF), BF),
    kt=((128, HALF), BF),
    vt=((128, HALF), BF),
    lo=((2, 64, HALF), BF),
    cc=((2, 256, HALF), BF),
    sp=((2, 2, 48, HALF), BF),
    sz=((2, 96, HALF), BF),
    dcb=((2, 256, HALF), BF),
    dcf=((2, 128, HALF), F32),
    rb=((2, 384, HALF), BF),
    sx=((2, 128, HALF), BF),
    ld=((2, 256, HALF), F32),
    gkv=((2, 256, HALF), BF),
    ao=((256, HALF), BF),
    qo=((256, HALF), BF),
    gs=((GROUPS, 256, 256), BF),
    gt=((GROUPS, 64, 1024), BF),
    rs=((GROUPS, 2, 4, 4, 32, 128), BF),
    ra=((GROUPS, 2, 3, 4, 32, 128), BF),
    tf=((GROUPS, 2, 4, 32, 128), F32),
    tb=((GROUPS, 2, 4, 32, 128), BF),
    rz=((GROUPS, 2, 3, 32, 128), BF),
    fo=((GROUPS, 64, 128), BF),
    ow=((D, 128), BF),
    gxf=((128, D), F32),
    gxs=((128, D), BF),
    gxr=((128, D), BF),
    pp=((592, 384), BF),
)


def kernel(x_h, q_h, v_h, w_h, g_h, p_h, att_o, gx_o, gq_o, gv_o, gw_o, *rest):
    s = dict(zip(SCRATCH, rest[: len(SCRATCH)]))
    ssem, rsem = rest[len(SCRATCH) :]
    xa, wv, qv, gv, kl, vl, kt, vt, lo = (s[n] for n in ("xa", "wv", "qv", "gv", "kl", "vl", "kt", "vt", "lo"))
    cc, sp, sz, dcb, dcf, rb, sx, ld = (s[n] for n in ("cc", "sp", "sz", "dcb", "dcf", "rb", "sx", "ld"))
    gkv, ao, qo, gs, gt = (s[n] for n in ("gkv", "ao", "qo", "gs", "gt"))
    rs, ra, tf, tb, rz, fo, ow = (s[n] for n in ("rs", "ra", "tf", "tb", "rz", "fo", "ow"))
    gxf, gxs, gxr, pp = (s[n] for n in ("gxf", "gxs", "gxr", "pp"))

    y = lax.axis_index("dp")
    ctx = lax.axis_index("ctx")
    core = ctx % 2
    xx = (ctx // 2) % 4
    zz = ctx // 8
    mate = (y, ctx + 1 - 2 * core)
    along_x = [(y, zz * 8 + flipped(xx, k) * 2 + core) for k in range(4)]
    cross_x = [(y, zz * 8 + flipped(xx, k) * 2 + 1 - core) for k in range(4)]
    along_z = [(y, flipped(zz, k) * 8 + xx * 2 + core) for k in range(4)]
    along_y = [(flipped(y, k), ctx) for k in range(4)]
    cross_y = [(flipped(y, k), mate[1]) for k in range(4)]
    mine = pl.multiple_of(core * HALF, HALF)
    theirs = pl.multiple_of((1 - core) * HALF, HALF)

    peers = [mate] + along_x[1:] + cross_x[1:] + along_z[1:] + along_y[1:] + cross_y[1:]
    barrier = pltpu.get_barrier_semaphore()
    for peer in peers:
        pl.semaphore_signal(barrier, inc=1, device_id=peer, device_id_type=MESH)

    count = [0]
    sent = []
    stored = []

    def remote(src, dst, device):
        at = count[0]
        count[0] += 1
        copy = pltpu.make_async_remote_copy(
            src_ref=src, dst_ref=dst, send_sem=ssem.at[at], recv_sem=rsem.at[at], device_id=device, device_id_type=MESH
        )
        copy.start()
        sent.append(copy)
        return copy

    def local(src, dst):
        at = count[0]
        count[0] += 1
        copy = pltpu.make_async_copy(src, dst, ssem.at[at])
        copy.start()
        return copy

    def arrive(copies):
        for copy in copies:
            copy.wait_recv()

    def cols(j):
        return pl.ds(j * GC, GC)

    in_x = local(x_h, xa.at[0:128])
    in_p = local(p_h, pp)
    in_v = [local(v_h.at[:, pl.ds(mine, HALF)], vl.at[0, 0:128]), local(v_h.at[:, pl.ds(theirs, HALF)], vt)]
    in_w = [
        [local(w_h.at[:, pl.ds(pl.multiple_of(side + j * GC, GC), GC)], wv.at[h, j]) for h, side in enumerate((mine, theirs))]
        for j in range(GROUPS)
    ]
    in_q = local(q_h.at[:, pl.ds(mine, HALF)], qv.at[0:128])
    in_g = local(g_h.at[:, pl.ds(mine, HALF)], gv.at[0:128])

    def pooled(kv, ref, h, j, rows_in):
        rows = nn(pp[0:112, 0:128], rows_in).astype(BF)
        sp[h, kv, :, cols(j)] = rows[64:112]
        if h == 0:
            ref[1, 128:192, cols(j)] = rows[0:64]
            lo[kv, 0:32, cols(j)] = rows[64:96]

    in_p.wait()
    for copy in in_v:
        copy.wait()
    for j in range(GROUPS):
        pooled(1, vl, 0, j, vl[0, 0:128, cols(j)])
        pooled(1, vl, 1, j, vt[:, cols(j)])
    in_x.wait()
    for j in range(GROUPS):
        for h in (0, 1):
            in_w[j][h].wait()
            keys = nn(xa[0:128, :], wv[h, j]).astype(BF)
            if h == 0:
                kl[0, 0:128, cols(j)] = keys
            else:
                kt[:, cols(j)] = keys
            pooled(0, kl, h, j, keys)

    pl.semaphore_wait(barrier, len(peers))

    def send_x(j):
        at = cols(j)
        copies = []
        for h, line in ((0, along_x), (1, cross_x)):
            first = sp.at[h, :, 0:32, at]
            second = sp.at[h, :, 32:48, at]
            copies.append(remote(first, cc.at[:, 32 * h : 32 * h + 32, at], line[1]))
            copies.append(remote(second, cc.at[:, 64 + 16 * h : 80 + 16 * h, at], line[2]))
            copies.append(remote(second, cc.at[:, 96 + 16 * h : 112 + 16 * h, at], line[3]))
        return copies

    fx = [send_x(0)]
    m_k = remote(kt, kl.at[1, 0:128], mate)
    m_v = remote(vt, vl.at[1, 0:128], mate)
    for j in range(1, GROUPS):
        fx.append(send_x(j))
    m_q = remote(q_h.at[:, pl.ds(theirs, HALF)], qv.at[128:256], mate)
    m_g = remote(g_h.at[:, pl.ds(theirs, HALF)], gv.at[128:256], mate)
    y_x = [None] + [remote(x_h, xa.at[k * 256 : k * 256 + 128], along_y[k]) for k in (1, 2, 3)]
    m_x = remote(x_h, xa.at[128:256], mate)

    arrive([m_k, m_v])
    for kv, ref in ((0, kl), (1, vl)):
        for j in range(GROUPS):
            rows = nn(pp[0:96, 0:128], ref[1, 0:128, cols(j)]).astype(BF)
            ref[0, 128:192, cols(j)] = rows[0:64]
            lo[kv, 32:64, cols(j)] = rows[64:96]

    def rise(j):
        arrive(fx[j])
        at = cols(j)
        for kv in (0, 1):
            rows = nn(pp[112:208, 0:64], lo[kv, :, at]) + nn(pp[112:208, 128:256], cc[kv, 0:128, at])
            sz[kv, :, at] = rows.astype(BF)
        return [
            remote(sz.at[:, 0:64, at], cc.at[:, 128:192, at], along_z[1]),
            remote(sz.at[:, 64:96, at], cc.at[:, 192:224, at], along_z[2]),
            remote(sz.at[:, 64:96, at], cc.at[:, 224:256, at], along_z[3]),
        ]

    def head(at):
        c = pl.ds(at, DH)
        q = qv[:, c]
        g = gv[:, c]
        ck = cc[0, :, c]
        cv = cc[1, :, c]
        rate = SCALE * math.log2(math.e)
        e1 = jnp.exp2(nt(q, ck) * rate)
        total = jnp.sum(e1, -1, keepdims=True)
        pair = [slice(0, 128), slice(128, 256)]
        e0 = [jnp.exp2(nt(q[pair[b]], kl[b, :, c]) * rate) for b in (0, 1)]
        total = total + jnp.concatenate([jnp.sum(e, -1, keepdims=True) for e in e0], 0)
        inverse = 1.0 / (total * 0.25)
        p1 = e1 * inverse
        p0 = [e0[b] * inverse[pair[b]] for b in (0, 1)]
        p1b = p1.astype(BF)
        p0b = [p.astype(BF) for p in p0]
        out = (nn(p1b, cv) + jnp.concatenate([nn(p0b[b], vl[b, :, c]) for b in (0, 1)], 0)) * 0.25
        ao[:, c] = out.astype(BF)
        delta = jnp.sum(g.astype(F32) * out, -1, keepdims=True)
        d1 = (p1 * (nt(g, cv) - delta)).astype(BF)
        d0 = [(p0[b] * (nt(g[pair[b]], vl[b, :, c]) - delta[pair[b]])).astype(BF) for b in (0, 1)]
        fold = SCALE * 0.25
        dq = (nn(d1, ck) + jnp.concatenate([nn(d0[b], kl[b, :, c]) for b in (0, 1)], 0)) * fold
        qo[:, c] = dq.astype(BF)
        dck = tn(d1, q) * fold
        dcv = tn(p1b, g) * 0.25
        dcf[0, :, c] = dck[0:128]
        dcf[1, :, c] = dcv[0:128]
        dcb[0, 128:256, c] = dck[128:256].astype(BF)
        dcb[1, 128:256, c] = dcv[128:256].astype(BF)
        for b in (0, 1):
            dk = tn(d0[b], q[pair[b]]) * fold
            dv = tn(p0b[b], g[pair[b]]) * 0.25
            ld[0, pair[b], c] = dk[0:128]
            ld[1, pair[b], c] = dv[0:128]
            other = slice(64 - 64 * b, 128 - 64 * b)
            rb[0, other, c] = dk[128:192].astype(BF)
            rb[1, other, c] = dv[128:192].astype(BF)

    def attend(j, copies):
        arrive(copies)

        def step(i, carry):
            head(pl.multiple_of(j * GC + i * DH, DH))
            return carry

        lax.fori_loop(0, GC // DH, step, 0)
        at = cols(j)
        return [
            remote(dcb.at[:, 128:192, at], rb.at[:, 256:320, at], along_z[1]),
            remote(dcb.at[:, 192:224, at], rb.at[:, 320:352, at], along_z[2]),
            remote(dcb.at[:, 224:256, at], rb.at[:, 352:384, at], along_z[3]),
        ]

    def return_x(j, copies):
        arrive(copies)
        at = cols(j)
        for kv in (0, 1):
            sx[kv, :, at] = (dcf[kv, :, at] + nn(pp[208:336, 0:128], rb[kv, 256:384, at])).astype(BF)
        return [
            remote(sx.at[:, 0:64, at], rb.at[:, 128:192, at], along_x[1]),
            remote(sx.at[:, 64:96, at], rb.at[:, 192:224, at], along_x[2]),
            remote(sx.at[:, 96:128, at], rb.at[:, 224:256, at], along_x[3]),
        ]

    def finish(j, copies):
        arrive(copies)
        at = cols(j)
        for kv in (0, 1):
            total = ld[kv, :, at] + nn(pp[336:592, :], rb[kv, :, at])
            gkv[kv, :, at] = total.astype(BF)
            if kv == 0:
                gs[j] = total.T.astype(BF)
        quarter = [pl.ds(pl.multiple_of(flipped(y, k) * 64, 64), 64) for k in range(4)]
        copies = [remote(gs.at[j, quarter[k]], gt.at[j, :, k * 256 : (k + 1) * 256], along_y[k]) for k in (1, 2, 3)]
        gt[j, :, 0:256] = gs[j, quarter[0], :]
        return copies

    def forward(k):
        arrive([y_x[k]])
        return remote(xa.at[k * 256 : k * 256 + 128], xa.at[k * 256 + 128 : k * 256 + 256], mate)

    lines = ((xx, along_x), (zz, along_z))

    def weights(j, copies):
        arrive(copies)

        def step(i, carry):
            part = nn(gt[j], xa[:, pl.ds(pl.multiple_of(i * 256, 256), 256)]).astype(BF)
            z_at = i // 2
            x_at = 2 * (i % 2)
            for n in (0, 1):
                rs[j, 0, x_at + n, z_at] = part[0:32, n * 128 : n * 128 + 128]
                rs[j, 1, z_at, x_at + n] = part[32:64, n * 128 : n * 128 + 128]
            return carry

        lax.fori_loop(0, 8, step, 0)
        return [
            remote(rs.at[j, d, flipped(lines[d][0], k)], ra.at[j, d, k - 1], lines[d][1][k]) for k in (1, 2, 3) for d in (0, 1)
        ]

    def second(j, copies):
        arrive(copies)
        copies = []
        for d in (0, 1):
            total = rs[j, d, lines[d][0]].astype(F32)
            for k in range(3):
                total = total + ra[j, d, k].astype(F32)
            tf[j, d] = total
            tb[j, d] = total.astype(BF)
            place, line = lines[1 - d]
            copies += [remote(tb.at[j, d, flipped(place, k)], rz.at[j, d, k - 1], line[k]) for k in (1, 2, 3)]
        return copies

    def third(j, copies):
        arrive(copies)
        for d in (0, 1):
            total = tf[j, d, lines[1 - d][0]]
            for k in range(3):
                total = total + rz[j, d, k].astype(F32)
            fo[j, d * 32 : d * 32 + 32] = total.astype(BF)
        at = pl.ds(pl.multiple_of(core * HALF + j * GC + y * 64, 64), 64)
        copies = [remote(fo.at[j], ow.at[at], along_y[k]) for k in (1, 2, 3)]
        copies += [remote(fo.at[j], ow.at[at], cross_y[k]) for k in range(4)]
        ow[at, :] = fo[j]
        return copies

    def assemble(j, copies):
        arrive(copies)
        for side in (0, 1):
            at = pl.ds(side * HALF + j * GC, GC)
            turned = ow[at, :].astype(F32).T
            gw_o[:, at] = jnp.where(core == 0, turned[0:64], turned[64:128])

    def give(staged, out):
        stored.append(local(staged.at[0:128], out.at[:, pl.ds(mine, HALF)]))
        return remote(staged.at[128:256], out.at[:, pl.ds(mine, HALF)], mate)

    def partial(i, carry):
        at = pl.ds(pl.multiple_of(i * 256, 256), 256)
        total = nt(gkv[0, :, cols(0)], wv[0, 0, at, :])
        for j in range(1, GROUPS):
            total = total + nt(gkv[0, :, cols(j)], wv[0, j, at, :])
        gxf[:, at] = total[0:128]
        gxs[:, at] = total[128:256].astype(BF)
        return carry

    fz = [rise(0), rise(1)]
    in_q.wait()
    in_g.wait()
    arrive([m_q, m_g])
    bz0 = attend(0, fz[0])
    fz.append(rise(2))
    bz1 = attend(1, fz[1])
    fz.append(rise(3))
    bx0 = return_x(0, bz0)
    bz2 = attend(2, fz[2])
    bx1 = return_x(1, bz1)
    gy0 = finish(0, bx0)
    bz3 = attend(3, fz[3])
    given = [give(ao, att_o), give(qo, gq_o)]
    bx2 = return_x(2, bz2)
    gy1 = finish(1, bx1)
    fw = [forward(1), forward(3)]
    bx3 = return_x(3, bz3)
    gy2 = finish(2, bx2)
    fw.append(forward(2))
    gy3 = finish(3, bx3)
    given.append(give(gkv.at[1], gv_o))
    arrive([m_x])
    arrive(fw)
    wa0 = weights(0, gy0)
    wa1 = weights(1, gy1)
    wa2 = weights(2, gy2)
    wa3 = weights(3, gy3)
    lax.fori_loop(0, 4, partial, 0)
    wb0 = second(0, wa0)
    wb1 = second(1, wa1)
    lax.fori_loop(4, 8, partial, 0)
    gxc = remote(gxs, gxr, mate)
    wb2 = second(2, wa2)
    wb3 = second(3, wa3)
    wc0 = third(0, wb0)
    wc1 = third(1, wb1)
    wc2 = third(2, wb2)
    wc3 = third(3, wb3)
    arrive([gxc])
    gx_o[...] = (gxf[...] + gxr[...].astype(F32)).astype(BF)
    assemble(0, wc0)
    assemble(1, wc1)
    assemble(2, wc2)
    assemble(3, wc3)
    arrive(given)
    for copy in stored:
        copy.wait()
    for copy in sent:
        copy.wait_send()


def hand_over(*refs):
    sources, outs, sem = refs[:5], refs[5:10], refs[10]
    copies = [pltpu.make_async_copy(src, out, sem.at[i]) for i, (src, out) in enumerate(zip(sources, outs))]
    for copy in copies:
        copy.start()
    for copy in copies:
        copy.wait()


def body(tokens, queries, values, key_weight, grad_out):
    anywhere = pl.BlockSpec(memory_space=pl.ANY)
    block = jax.ShapeDtypeStruct((TOK, D), BF)
    shapes = [block] * 4 + [jax.ShapeDtypeStruct((64, D), F32)]
    held = [pltpu.VMEM(shape.shape, shape.dtype) for shape in shapes]
    results = pl.pallas_call(
        kernel,
        out_shape=held,
        in_specs=[anywhere] * 6,
        out_specs=[pl.BlockSpec(memory_space=pltpu.VMEM)] * 5,
        scratch_shapes=[pltpu.VMEM(shape, dtype) for shape, dtype in SCRATCH.values()]
        + [pltpu.SemaphoreType.DMA((N_SEM,)), pltpu.SemaphoreType.DMA((N_SEM,))],
        compiler_params=pltpu.CompilerParams(
            collective_id=0, has_side_effects=True, vmem_limit_bytes=56 * 1024 * 1024
        ),
        name="hierarchical_attention",
    )(tokens[0], queries[0], values[0], key_weight, grad_out[0], jnp.asarray(matrices(), BF))
    att, gx, gq, gv, gw = pl.pallas_call(
        hand_over,
        out_shape=shapes,
        in_specs=[pl.BlockSpec(memory_space=pltpu.VMEM)] * 5,
        out_specs=[anywhere] * 5,
        scratch_shapes=[pltpu.SemaphoreType.DMA((5,))],
        name="hand_over",
    )(*[pltpu.with_memory_space_constraint(r, pltpu.VMEM) for r in results])
    return att[None], gx[None], gq[None], gv[None], gw


def solution(mesh):
    split = P("dp", "ctx", None)
    return jax.shard_map(
        body,
        mesh=mesh,
        in_specs=(split, split, split, P(), split),
        out_specs=(split, split, split, split, P("ctx", None)),
        check_vma=False,
    )
```

time: 84.2 us -> 71.8 us (0.85)
  local copies, waits for them, and re-layouts: 7.52 us -> 0 us
  Pallas kernels: 74 us -> 71 us
  other arithmetic: 1.78 us -> 0 us
    unnamed x4 -> x0, local copies, waits for them, and re-layouts: 7.52 us -> none
    pallas_call x1 -> x2, Pallas kernels: 74 us -> 71 us  [the longest x1 69.5 us: body(): pl.pallas_call(kernel, out_shape=held, in_specs=[anywhere] * 6, out_specs...]
    convert_element_type x1 -> x0, other arithmetic: 1.78 us -> none  [body(): return (att[None], gx[None], gq[None], gv[None], gw.astype(F32))]
where the time goes in v1:
time: 71.8 us; the launch traced here: 71.7 us
  Pallas kernels  71 us (99%)
    pallas_call x1, Pallas kernels, body(): pl.pallas_call(kernel, out_shape=held, in_specs=[anywhere] * 6, out_specs...  69.5 us
    pallas_call x1, Pallas kernels, body(): pl.pallas_call(hand_over, out_shape=shapes, in_specs=[pl.BlockSpec(memory...  1.53 us

profile of v1, /device:TPU:1, one launch (start us, length us, event | category | flops | bytes accessed | tf_op | source)
XLA Modules:
  0.0 71.7 jit_solution(4009393036621239114)
XLA Ops:
  0.6 69.5 %hierarchical_attention.1 = (bf16[128,2048]{1,0:T(8,128)(2,1)S(1)}, bf16[128,2048]{1,0:T(8,128)(2,1)S(1)}, bf16[128,2048]{1,0:T(8,128)(2,1)S(1)}, bf16[128,2048]{1,0:T(8,128)(2,1)S(1)}, f32[64,2048]{1,0:T(8,128)S(1)}) custom-call(bf16[128,2048]{1,0:T(8,128)(2,1)} %bitcast.8, bf16[128,2048]{1,0:T(8,128)(2,1)} %bitcast.9, bf16[128,2048]{1,0:T(8,128)(2,1)} %bitcast.10, ...), custom_call_target="tpu_custom_call" | custom-call | tf_op jit(solution)/shard_map/hierarchical_attention/pallas_call | solution.py:462
  70.1 1.5 %hand_over.1 = (bf16[128,2048]{1,0:T(8,128)(2,1)}, bf16[128,2048]{1,0:T(8,128)(2,1)}, bf16[128,2048]{1,0:T(8,128)(2,1)}, bf16[128,2048]{1,0:T(8,128)(2,1)}, f32[64,2048]{1,0:T(8,128)}) custom-call(bf16[128,2048]{1,0:T(8,128)(2,1)S(1)} %get-tuple-element.15.refs_0_, bf16[128,2048]{1,0:T(8,128)(2,1)S(1)} %get-tuple-element.16.refs_1_, ...), custom_call_target="tpu_custom_call" | custom-call | tf_op jit(solution)/shard_map/hand_over/pallas_call | solution.py:474

commit v2 on v1

--- a/solution.py
+++ b/solution.py
@@ -14,11 +14,14 @@
 HALF = D // 2
 GROUPS = 4
 GC = HALF // GROUPS
+HEADS = 8
+PARTS = ((0, 6), (6, 8))
 SCALE = DH ** (-0.5)
 BF = jnp.bfloat16
 F32 = jnp.float32
 MESH = pl.DeviceIdType.MESH
-N_SEM = 208
+SENDS = 48
+LANDINGS = 60
 
 
 def matrices():
@@ -97,15 +100,23 @@
     gkv=((2, 256, HALF), BF),
     ao=((256, HALF), BF),
     qo=((256, HALF), BF),
-    gs=((GROUPS, 256, 256), BF),
-    gt=((GROUPS, 64, 1024), BF),
-    rs=((GROUPS, 2, 4, 4, 32, 128), BF),
-    ra=((GROUPS, 2, 3, 4, 32, 128), BF),
-    tf=((GROUPS, 2, 4, 32, 128), F32),
-    tb=((GROUPS, 2, 4, 32, 128), BF),
-    rz=((GROUPS, 2, 3, 32, 128), BF),
-    fo=((GROUPS, 64, 128), BF),
-    ow=((D, 128), BF),
+    gs=((HALF, 256), BF),
+    gt0=((192, 1024), BF),
+    gt1=((64, 1024), BF),
+    rs0=((2, 4, 4, 96, 128), BF),
+    rs1=((2, 4, 4, 32, 128), BF),
+    ra0=((2, 3, 4, 96, 128), BF),
+    ra1=((2, 3, 4, 32, 128), BF),
+    tf0=((2, 4, 96, 128), F32),
+    tf1=((2, 4, 32, 128), F32),
+    tb0=((2, 4, 96, 128), BF),
+    tb1=((2, 4, 32, 128), BF),
+    rz0=((2, 3, 96, 128), BF),
+    rz1=((2, 3, 32, 128), BF),
+    fo0=((192, 128), BF),
+    fo1=((64, 128), BF),
+    ow0=((2, 4, 192, 128), BF),
+    ow1=((2, 4, 64, 128), BF),
     gxf=((128, D), F32),
     gxs=((128, D), BF),
     gxr=((128, D), BF),
@@ -118,8 +129,8 @@
     ssem, rsem = rest[len(SCRATCH) :]
     xa, wv, qv, gv, kl, vl, kt, vt, lo = (s[n] for n in ("xa", "wv", "qv", "gv", "kl", "vl", "kt", "vt", "lo"))
     cc, sp, sz, dcb, dcf, rb, sx, ld = (s[n] for n in ("cc", "sp", "sz", "dcb", "dcf", "rb", "sx", "ld"))
-    gkv, ao, qo, gs, gt = (s[n] for n in ("gkv", "ao", "qo", "gs", "gt"))
-    rs, ra, tf, tb, rz, fo, ow = (s[n] for n in ("rs", "ra", "tf", "tb", "rz", "fo", "ow"))
+    gkv, ao, qo, gs = (s[n] for n in ("gkv", "ao", "qo", "gs"))
+    gt, rs, ra, tf, tb, rz, fo, ow = ([s[n + p] for p in "01"] for n in ("gt", "rs", "ra", "tf", "tb", "rz", "fo", "ow"))
     gxf, gxs, gxr, pp = (s[n] for n in ("gxf", "gxs", "gxr", "pp"))
 
     y = lax.axis_index("dp")
@@ -142,18 +153,41 @@
         pl.semaphore_signal(barrier, inc=1, device_id=peer, device_id_type=MESH)
 
     count = [0]
+    arrivals = [0]
     sent = []
     stored = []
 
+    class Landing:
+        def __init__(self, whole, send_at):
+            self.copy = pltpu.make_async_remote_copy(
+                src_ref=whole,
+                dst_ref=whole,
+                send_sem=ssem.at[send_at],
+                recv_sem=rsem.at[arrivals[0]],
+                device_id=mate,
+                device_id_type=MESH,
+            )
+            arrivals[0] += 1
+
+    def start(src, dst, device, send_at, recv_at):
+        pltpu.make_async_remote_copy(
+            src_ref=src, dst_ref=dst, send_sem=ssem.at[send_at], recv_sem=rsem.at[recv_at], device_id=device, device_id_type=MESH
+        ).start()
+
+    class Route:
+        def __init__(self, total):
+            self.at = count[0]
+            count[0] += 1
+            sent.append((total, self.at))
+
+        def send(self, whole, messages):
+            landing = Landing(whole, self.at)
+            for src, dst, device in messages:
+                start(src, dst, device, self.at, arrivals[0] - 1)
+            return landing
+
     def remote(src, dst, device):
-        at = count[0]
-        count[0] += 1
-        copy = pltpu.make_async_remote_copy(
-            src_ref=src, dst_ref=dst, send_sem=ssem.at[at], recv_sem=rsem.at[at], device_id=device, device_id_type=MESH
-        )
-        copy.start()
-        sent.append(copy)
-        return copy
+        return Route(dst).send(dst, [(src, dst, device)])
 
     def local(src, dst):
         at = count[0]
@@ -164,10 +198,13 @@
 
     def arrive(copies):
         for copy in copies:
-            copy.wait_recv()
+            copy.copy.wait_recv()
 
     def cols(j):
         return pl.ds(j * GC, GC)
+
+    def head_cols(i):
+        return pl.ds(i * DH, DH)
 
     in_x = local(x_h, xa.at[0:128])
     in_p = local(p_h, pp)
@@ -204,26 +241,28 @@
             pooled(0, kl, h, j, keys)
 
     pl.semaphore_wait(barrier, len(peers))
-
-    def send_x(j):
-        at = cols(j)
-        copies = []
+    fx_route, fz_route = Route(cc.at[:, 0:128]), Route(cc.at[:, 128:256])
+    bx_route, bz_route = Route(rb.at[:, 128:256]), Route(rb.at[:, 256:384])
+
+    def send_x(i):
+        at = head_cols(i)
+        messages = []
         for h, line in ((0, along_x), (1, cross_x)):
             first = sp.at[h, :, 0:32, at]
             second = sp.at[h, :, 32:48, at]
-            copies.append(remote(first, cc.at[:, 32 * h : 32 * h + 32, at], line[1]))
-            copies.append(remote(second, cc.at[:, 64 + 16 * h : 80 + 16 * h, at], line[2]))
-            copies.append(remote(second, cc.at[:, 96 + 16 * h : 112 + 16 * h, at], line[3]))
-        return copies
+            messages.append((first, cc.at[:, 32 * h : 32 * h + 32, at], line[1]))
+            messages.append((second, cc.at[:, 64 + 16 * h : 80 + 16 * h, at], line[2]))
+            messages.append((second, cc.at[:, 96 + 16 * h : 112 + 16 * h, at], line[3]))
+        return fx_route.send(cc.at[:, 0:128, at], messages)
 
     fx = [send_x(0)]
     m_k = remote(kt, kl.at[1, 0:128], mate)
     m_v = remote(vt, vl.at[1, 0:128], mate)
-    for j in range(1, GROUPS):
-        fx.append(send_x(j))
+    for i in range(1, HEADS):
+        fx.append(send_x(i))
+    y_x = {k: remote(x_h, xa.at[k * 256 : k * 256 + 128], along_y[k]) for k in (1, 3)}
     m_q = remote(q_h.at[:, pl.ds(theirs, HALF)], qv.at[128:256], mate)
     m_g = remote(g_h.at[:, pl.ds(theirs, HALF)], gv.at[128:256], mate)
-    y_x = [None] + [remote(x_h, xa.at[k * 256 : k * 256 + 128], along_y[k]) for k in (1, 2, 3)]
     m_x = remote(x_h, xa.at[128:256], mate)
 
     arrive([m_k, m_v])
@@ -233,20 +272,22 @@
             ref[0, 128:192, cols(j)] = rows[0:64]
             lo[kv, 32:64, cols(j)] = rows[64:96]
 
-    def rise(j):
-        arrive(fx[j])
-        at = cols(j)
+    def rise(i):
+        arrive([fx[i]])
+        at = head_cols(i)
         for kv in (0, 1):
             rows = nn(pp[112:208, 0:64], lo[kv, :, at]) + nn(pp[112:208, 128:256], cc[kv, 0:128, at])
             sz[kv, :, at] = rows.astype(BF)
-        return [
-            remote(sz.at[:, 0:64, at], cc.at[:, 128:192, at], along_z[1]),
-            remote(sz.at[:, 64:96, at], cc.at[:, 192:224, at], along_z[2]),
-            remote(sz.at[:, 64:96, at], cc.at[:, 224:256, at], along_z[3]),
-        ]
-
-    def head(at):
-        c = pl.ds(at, DH)
+        return fz_route.send(
+            cc.at[:, 128:256, at],
+            [
+                (sz.at[:, 0:64, at], cc.at[:, 128:192, at], along_z[1]),
+                (sz.at[:, 64:96, at], cc.at[:, 192:224, at], along_z[2]),
+                (sz.at[:, 64:96, at], cc.at[:, 224:256, at], along_z[3]),
+            ],
+        )
+
+    def head(c):
         q = qv[:, c]
         g = gv[:, c]
         ck = cc[0, :, c]
@@ -285,100 +326,121 @@
             rb[0, other, c] = dk[128:192].astype(BF)
             rb[1, other, c] = dv[128:192].astype(BF)
 
-    def attend(j, copies):
-        arrive(copies)
-
-        def step(i, carry):
-            head(pl.multiple_of(j * GC + i * DH, DH))
-            return carry
-
-        lax.fori_loop(0, GC // DH, step, 0)
-        at = cols(j)
-        return [
-            remote(dcb.at[:, 128:192, at], rb.at[:, 256:320, at], along_z[1]),
-            remote(dcb.at[:, 192:224, at], rb.at[:, 320:352, at], along_z[2]),
-            remote(dcb.at[:, 224:256, at], rb.at[:, 352:384, at], along_z[3]),
-        ]
-
-    def return_x(j, copies):
-        arrive(copies)
-        at = cols(j)
+    def attend(i, landing):
+        arrive([landing])
+        at = head_cols(i)
+        head(at)
+        return bz_route.send(
+            rb.at[:, 256:384, at],
+            [
+                (dcb.at[:, 128:192, at], rb.at[:, 256:320, at], along_z[1]),
+                (dcb.at[:, 192:224, at], rb.at[:, 320:352, at], along_z[2]),
+                (dcb.at[:, 224:256, at], rb.at[:, 352:384, at], along_z[3]),
+            ],
+        )
+
+    def return_x(i, landing):
+        arrive([landing])
+        at = head_cols(i)
         for kv in (0, 1):
             sx[kv, :, at] = (dcf[kv, :, at] + nn(pp[208:336, 0:128], rb[kv, 256:384, at])).astype(BF)
-        return [
-            remote(sx.at[:, 0:64, at], rb.at[:, 128:192, at], along_x[1]),
-            remote(sx.at[:, 64:96, at], rb.at[:, 192:224, at], along_x[2]),
-            remote(sx.at[:, 96:128, at], rb.at[:, 224:256, at], along_x[3]),
-        ]
-
-    def finish(j, copies):
-        arrive(copies)
-        at = cols(j)
+        return bx_route.send(
+            rb.at[:, 128:256, at],
+            [
+                (sx.at[:, 0:64, at], rb.at[:, 128:192, at], along_x[1]),
+                (sx.at[:, 64:96, at], rb.at[:, 192:224, at], along_x[2]),
+                (sx.at[:, 96:128, at], rb.at[:, 224:256, at], along_x[3]),
+            ],
+        )
+
+    def finish(i, landing):
+        arrive([landing])
+        at = head_cols(i)
         for kv in (0, 1):
             total = ld[kv, :, at] + nn(pp[336:592, :], rb[kv, :, at])
             gkv[kv, :, at] = total.astype(BF)
             if kv == 0:
-                gs[j] = total.T.astype(BF)
-        quarter = [pl.ds(pl.multiple_of(flipped(y, k) * 64, 64), 64) for k in range(4)]
-        copies = [remote(gs.at[j, quarter[k]], gt.at[j, :, k * 256 : (k + 1) * 256], along_y[k]) for k in (1, 2, 3)]
-        gt[j, :, 0:256] = gs[j, quarter[0], :]
-        return copies
+                gs[at, :] = total.T.astype(BF)
+
+    def send_y(p):
+        first, last = PARTS[p]
+        each = (last - first) * 32
+        quarter = [pl.ds(pl.multiple_of(first * DH + flipped(y, k) * each, 64), each) for k in range(4)]
+        landing = Route(gt[p].at[:, 256:1024]).send(
+            gt[p].at[:, 256:1024],
+            [(gs.at[quarter[k]], gt[p].at[:, k * 256 : (k + 1) * 256], along_y[k]) for k in (1, 2, 3)],
+        )
+        gt[p][:, 0:256] = gs[quarter[0], :]
+        return landing
 
     def forward(k):
         arrive([y_x[k]])
-        return remote(xa.at[k * 256 : k * 256 + 128], xa.at[k * 256 + 128 : k * 256 + 256], mate)
+        rows = 0 if k == 1 else 64
+        ahead = remote(xa.at[k * 256 + rows : k * 256 + rows + 64], xa.at[512 + rows : 512 + rows + 64], along_y[4 - k])
+        return remote(xa.at[k * 256 : k * 256 + 128], xa.at[k * 256 + 128 : k * 256 + 256], mate), ahead
 
     lines = ((xx, along_x), (zz, along_z))
 
-    def weights(j, copies):
-        arrive(copies)
+    def weights(p, landing):
+        arrive([landing])
+        each = rs[p].shape[3]
 
         def step(i, carry):
-            part = nn(gt[j], xa[:, pl.ds(pl.multiple_of(i * 256, 256), 256)]).astype(BF)
+            part = nn(gt[p][...], xa[:, pl.ds(pl.multiple_of(i * 256, 256), 256)]).astype(BF)
             z_at = i // 2
             x_at = 2 * (i % 2)
             for n in (0, 1):
-                rs[j, 0, x_at + n, z_at] = part[0:32, n * 128 : n * 128 + 128]
-                rs[j, 1, z_at, x_at + n] = part[32:64, n * 128 : n * 128 + 128]
+                rs[p][0, x_at + n, z_at] = part[0:each, n * 128 : n * 128 + 128]
+                rs[p][1, z_at, x_at + n] = part[each : 2 * each, n * 128 : n * 128 + 128]
             return carry
 
         lax.fori_loop(0, 8, step, 0)
-        return [
-            remote(rs.at[j, d, flipped(lines[d][0], k)], ra.at[j, d, k - 1], lines[d][1][k]) for k in (1, 2, 3) for d in (0, 1)
-        ]
-
-    def second(j, copies):
-        arrive(copies)
-        copies = []
+        return Route(ra[p]).send(
+            ra[p],
+            [
+                (rs[p].at[d, flipped(lines[d][0], k)], ra[p].at[d, k - 1], lines[d][1][k])
+                for k in (2, 1, 3)
+                for d in (0, 1)
+            ],
+        )
+
+    def second(p, landing):
+        arrive([landing])
+        messages = []
         for d in (0, 1):
-            total = rs[j, d, lines[d][0]].astype(F32)
+            total = rs[p][d, lines[d][0]].astype(F32)
             for k in range(3):
-                total = total + ra[j, d, k].astype(F32)
-            tf[j, d] = total
-            tb[j, d] = total.astype(BF)
+                total = total + ra[p][d, k].astype(F32)
+            tf[p][d] = total
+            tb[p][d] = total.astype(BF)
             place, line = lines[1 - d]
-            copies += [remote(tb.at[j, d, flipped(place, k)], rz.at[j, d, k - 1], line[k]) for k in (1, 2, 3)]
-        return copies
-
-    def third(j, copies):
-        arrive(copies)
+            messages += [(tb[p].at[d, flipped(place, k)], rz[p].at[d, k - 1], line[k]) for k in (2, 1, 3)]
+        return Route(rz[p]).send(rz[p], messages)
+
+    def third(p, landing):
+        arrive([landing])
+        each = rs[p].shape[3]
         for d in (0, 1):
-            total = tf[j, d, lines[1 - d][0]]
+            total = tf[p][d, lines[1 - d][0]]
             for k in range(3):
-                total = total + rz[j, d, k].astype(F32)
-            fo[j, d * 32 : d * 32 + 32] = total.astype(BF)
-        at = pl.ds(pl.multiple_of(core * HALF + j * GC + y * 64, 64), 64)
-        copies = [remote(fo.at[j], ow.at[at], along_y[k]) for k in (1, 2, 3)]
-        copies += [remote(fo.at[j], ow.at[at], cross_y[k]) for k in range(4)]
-        ow[at, :] = fo[j]
-        return copies
-
-    def assemble(j, copies):
-        arrive(copies)
+                total = total + rz[p][d, k].astype(F32)
+            fo[p][d * each : d * each + each] = total.astype(BF)
+        whole = xa.at[0 : 7 * each, 0:256]
+        landing = Route(whole).send(
+            whole,
+            [(fo[p], ow[p].at[core, y], along_y[k]) for k in (2, 1, 3)]
+            + [(fo[p], ow[p].at[core, y], cross_y[k]) for k in (2, 1, 3, 0)],
+        )
+        ow[p][core, y] = fo[p][...]
+        return landing
+
+    def assemble(p, landing):
+        arrive([landing])
+        first, last = PARTS[p]
+        wide = (last - first) * DH
         for side in (0, 1):
-            at = pl.ds(side * HALF + j * GC, GC)
-            turned = ow[at, :].astype(F32).T
-            gw_o[:, at] = jnp.where(core == 0, turned[0:64], turned[64:128])
+            turned = ow[p][side].astype(F32).reshape(wide, 128).T
+            gw_o[:, pl.ds(side * HALF + first * DH, wide)] = jnp.where(core == 0, turned[0:64], turned[64:128])
 
     def give(staged, out):
         stored.append(local(staged.at[0:128], out.at[:, pl.ds(mine, HALF)]))
@@ -393,56 +455,63 @@
         gxs[:, at] = total[128:256].astype(BF)
         return carry
 
-    fz = [rise(0), rise(1)]
+    fz = [rise(i) for i in range(4)]
     in_q.wait()
     in_g.wait()
     arrive([m_q, m_g])
-    bz0 = attend(0, fz[0])
-    fz.append(rise(2))
-    bz1 = attend(1, fz[1])
-    fz.append(rise(3))
-    bx0 = return_x(0, bz0)
-    bz2 = attend(2, fz[2])
-    bx1 = return_x(1, bz1)
-    gy0 = finish(0, bx0)
-    bz3 = attend(3, fz[3])
+    bz, bx = [], []
+    for i in range(4):
+        bz.append(attend(i, fz[i]))
+        fz.append(rise(4 + i))
+    f1, a1 = forward(1)
+    f3, a3 = forward(3)
+    bz.append(attend(4, fz[4]))
+    bz.append(attend(5, fz[5]))
+    bx.append(return_x(0, bz[0]))
+    bx.append(return_x(1, bz[1]))
+    bz.append(attend(6, fz[6]))
+    bx.append(return_x(2, bz[2]))
+    bz.append(attend(7, fz[7]))
     given = [give(ao, att_o), give(qo, gq_o)]
-    bx2 = return_x(2, bz2)
-    gy1 = finish(1, bx1)
-    fw = [forward(1), forward(3)]
-    bx3 = return_x(3, bz3)
-    gy2 = finish(2, bx2)
-    fw.append(forward(2))
-    gy3 = finish(3, bx3)
+    bx.append(return_x(3, bz[3]))
+    bx.append(return_x(4, bz[4]))
+    finish(0, bx[0])
+    bx.append(return_x(5, bz[5]))
+    finish(1, bx[1])
+    bx.append(return_x(6, bz[6]))
+    finish(2, bx[2])
+    bx.append(return_x(7, bz[7]))
+    arrive([a1, a3])
+    f2 = remote(xa.at[512:640], xa.at[640:768], mate)
+    finish(3, bx[3])
+    finish(4, bx[4])
+    finish(5, bx[5])
+    gy0 = send_y(0)
+    finish(6, bx[6])
+    finish(7, bx[7])
+    gy1 = send_y(1)
     given.append(give(gkv.at[1], gv_o))
-    arrive([m_x])
-    arrive(fw)
+    arrive([m_x, f1, f3, f2])
     wa0 = weights(0, gy0)
     wa1 = weights(1, gy1)
-    wa2 = weights(2, gy2)
-    wa3 = weights(3, gy3)
-    lax.fori_loop(0, 4, partial, 0)
     wb0 = second(0, wa0)
+    lax.fori_loop(0, 8, partial, 0)
+    gxc = remote(gxs, gxr, mate)
     wb1 = second(1, wa1)
-    lax.fori_loop(4, 8, partial, 0)
-    gxc = remote(gxs, gxr, mate)
-    wb2 = second(2, wa2)
-    wb3 = second(3, wa3)
     wc0 = third(0, wb0)
     wc1 = third(1, wb1)
-    wc2 = third(2, wb2)
-    wc3 = third(3, wb3)
     arrive([gxc])
     gx_o[...] = (gxf[...] + gxr[...].astype(F32)).astype(BF)
     assemble(0, wc0)
     assemble(1, wc1)
-    assemble(2, wc2)
-    assemble(3, wc3)
     arrive(given)
+    assert count[0] <= SENDS and arrivals[0] <= LANDINGS, (count, arrivals)
     for copy in stored:
         copy.wait()
-    for copy in sent:
-        copy.wait_send()
+    for total, at in sent:
+        pltpu.make_async_remote_copy(
+            src_ref=total, dst_ref=total, send_sem=ssem.at[at], recv_sem=rsem.at[0], device_id=mate, device_id_type=MESH
+        ).wait_send()
 
 
 def hand_over(*refs):
@@ -465,7 +534,7 @@
         in_specs=[anywhere] * 6,
         out_specs=[pl.BlockSpec(memory_space=pltpu.VMEM)] * 5,
         scratch_shapes=[pltpu.VMEM(shape, dtype) for shape, dtype in SCRATCH.values()]
-        + [pltpu.SemaphoreType.DMA((N_SEM,)), pltpu.SemaphoreType.DMA((N_SEM,))],
+        + [pltpu.SemaphoreType.DMA((SENDS,)), pltpu.SemaphoreType.DMA((LANDINGS,))],
         compiler_params=pltpu.CompilerParams(
             collective_id=0, has_side_effects=True, vmem_limit_bytes=56 * 1024 * 1024
         ),

time: 71.8 us -> 66.8 us (0.930)
  Pallas kernels: 71 us -> 65.9 us
    pallas_call x1, Pallas kernels: 69.5 us -> 64.4 us  [body(): pl.pallas_call(kernel, out_shape=held, in_specs=[anywhere] * 6, out_specs...]
where the time goes in v2:
time: 66.8 us; the launch traced here: 66.7 us
  Pallas kernels  65.9 us (99%)
  between operations  0.8 us (1%)
    pallas_call x1, Pallas kernels, body(): pl.pallas_call(kernel, out_shape=held, in_specs=[anywhere] * 6, out_specs...  64.4 us
    pallas_call x1, Pallas kernels, body(): pl.pallas_call(hand_over, out_shape=shapes, in_specs=[pl.BlockSpec(memory...  1.53 us

profile of v2, /device:TPU:1, one launch (start us, length us, event | category | flops | bytes accessed | tf_op | source)
XLA Modules:
  0.0 66.7 jit_solution(17041423612125052733)
XLA Ops:
  0.6 64.4 %hierarchical_attention.1 = (bf16[128,2048]{1,0:T(8,128)(2,1)S(1)}, bf16[128,2048]{1,0:T(8,128)(2,1)S(1)}, bf16[128,2048]{1,0:T(8,128)(2,1)S(1)}, bf16[128,2048]{1,0:T(8,128)(2,1)S(1)}, f32[64,2048]{1,0:T(8,128)S(1)}) custom-call(bf16[128,2048]{1,0:T(8,128)(2,1)} %bitcast.8, bf16[128,2048]{1,0:T(8,128)(2,1)} %bitcast.9, bf16[128,2048]{1,0:T(8,128)(2,1)} %bitcast.10, ...), custom_call_target="tpu_custom_call" | custom-call | tf_op jit(solution)/shard_map/hierarchical_attention/pallas_call | solution.py:531
  65.0 1.5 %hand_over.1 = (bf16[128,2048]{1,0:T(8,128)(2,1)}, bf16[128,2048]{1,0:T(8,128)(2,1)}, bf16[128,2048]{1,0:T(8,128)(2,1)}, bf16[128,2048]{1,0:T(8,128)(2,1)}, f32[64,2048]{1,0:T(8,128)}) custom-call(bf16[128,2048]{1,0:T(8,128)(2,1)S(1)} %get-tuple-element.15.refs_0_, bf16[128,2048]{1,0:T(8,128)(2,1)S(1)} %get-tuple-element.16.refs_1_, ...), custom_call_target="tpu_custom_call" | custom-call | tf_op jit(solution)/shard_map/hand_over/pallas_call | solution.py:543

commit v3 on v2

--- a/solution.py
+++ b/solution.py
@@ -15,12 +15,12 @@
 GROUPS = 4
 GC = HALF // GROUPS
 HEADS = 8
-PARTS = ((0, 6), (6, 8))
+PARTS = ((0, 4), (4, 7), (7, 8))
 SCALE = DH ** (-0.5)
 BF = jnp.bfloat16
 F32 = jnp.float32
 MESH = pl.DeviceIdType.MESH
-SENDS = 48
+SENDS = 52
 LANDINGS = 60
 
 
@@ -101,22 +101,30 @@
     ao=((256, HALF), BF),
     qo=((256, HALF), BF),
     gs=((HALF, 256), BF),
-    gt0=((192, 1024), BF),
-    gt1=((64, 1024), BF),
-    rs0=((2, 4, 4, 96, 128), BF),
-    rs1=((2, 4, 4, 32, 128), BF),
-    ra0=((2, 3, 4, 96, 128), BF),
-    ra1=((2, 3, 4, 32, 128), BF),
-    tf0=((2, 4, 96, 128), F32),
-    tf1=((2, 4, 32, 128), F32),
-    tb0=((2, 4, 96, 128), BF),
-    tb1=((2, 4, 32, 128), BF),
-    rz0=((2, 3, 96, 128), BF),
-    rz1=((2, 3, 32, 128), BF),
-    fo0=((192, 128), BF),
-    fo1=((64, 128), BF),
-    ow0=((2, 4, 192, 128), BF),
-    ow1=((2, 4, 64, 128), BF),
+    gt0=((128, 1024), BF),
+    gt1=((96, 1024), BF),
+    gt2=((32, 1024), BF),
+    rs0=((2, 4, 4, 64, 128), BF),
+    rs1=((2, 4, 4, 48, 128), BF),
+    rs2=((2, 4, 4, 16, 128), BF),
+    ra0=((2, 3, 4, 64, 128), BF),
+    ra1=((2, 3, 4, 48, 128), BF),
+    ra2=((2, 3, 4, 16, 128), BF),
+    tf0=((2, 4, 64, 128), F32),
+    tf1=((2, 4, 48, 128), F32),
+    tf2=((2, 4, 16, 128), F32),
+    tb0=((2, 4, 64, 128), BF),
+    tb1=((2, 4, 48, 128), BF),
+    tb2=((2, 4, 16, 128), BF),
+    rz0=((2, 3, 64, 128), BF),
+    rz1=((2, 3, 48, 128), BF),
+    rz2=((2, 3, 16, 128), BF),
+    fo0=((128, 128), BF),
+    fo1=((96, 128), BF),
+    fo2=((32, 128), BF),
+    ow0=((2, 4, 128, 128), BF),
+    ow1=((2, 4, 96, 128), BF),
+    ow2=((2, 4, 32, 128), BF),
     gxf=((128, D), F32),
     gxs=((128, D), BF),
     gxr=((128, D), BF),
@@ -130,7 +138,7 @@
     xa, wv, qv, gv, kl, vl, kt, vt, lo = (s[n] for n in ("xa", "wv", "qv", "gv", "kl", "vl", "kt", "vt", "lo"))
     cc, sp, sz, dcb, dcf, rb, sx, ld = (s[n] for n in ("cc", "sp", "sz", "dcb", "dcf", "rb", "sx", "ld"))
     gkv, ao, qo, gs = (s[n] for n in ("gkv", "ao", "qo", "gs"))
-    gt, rs, ra, tf, tb, rz, fo, ow = ([s[n + p] for p in "01"] for n in ("gt", "rs", "ra", "tf", "tb", "rz", "fo", "ow"))
+    gt, rs, ra, tf, tb, rz, fo, ow = ([s[n + p] for p in "012"] for n in ("gt", "rs", "ra", "tf", "tb", "rz", "fo", "ow"))
     gxf, gxs, gxr, pp = (s[n] for n in ("gxf", "gxs", "gxr", "pp"))
 
     y = lax.axis_index("dp")
@@ -365,7 +373,7 @@
     def send_y(p):
         first, last = PARTS[p]
         each = (last - first) * 32
-        quarter = [pl.ds(pl.multiple_of(first * DH + flipped(y, k) * each, 64), each) for k in range(4)]
+        quarter = [pl.ds(pl.multiple_of(first * DH + flipped(y, k) * each, 32), each) for k in range(4)]
         landing = Route(gt[p].at[:, 256:1024]).send(
             gt[p].at[:, 256:1024],
             [(gs.at[quarter[k]], gt[p].at[:, k * 256 : (k + 1) * 256], along_y[k]) for k in (1, 2, 3)],
@@ -385,16 +393,13 @@
         arrive([landing])
         each = rs[p].shape[3]
 
-        def step(i, carry):
-            part = nn(gt[p][...], xa[:, pl.ds(pl.multiple_of(i * 256, 256), 256)]).astype(BF)
-            z_at = i // 2
-            x_at = 2 * (i % 2)
+        columns = gt[p][...]
+        for i in range(8):
+            part = nn(columns, xa[:, i * 256 : i * 256 + 256]).astype(BF)
             for n in (0, 1):
-                rs[p][0, x_at + n, z_at] = part[0:each, n * 128 : n * 128 + 128]
-                rs[p][1, z_at, x_at + n] = part[each : 2 * each, n * 128 : n * 128 + 128]
-            return carry
-
-        lax.fori_loop(0, 8, step, 0)
+                x_at = 2 * (i % 2) + n
+                rs[p][0, x_at, i // 2] = part[0:each, n * 128 : n * 128 + 128]
+                rs[p][1, i // 2, x_at] = part[each : 2 * each, n * 128 : n * 128 + 128]
         return Route(ra[p]).send(
             ra[p],
             [
@@ -446,64 +451,68 @@
         stored.append(local(staged.at[0:128], out.at[:, pl.ds(mine, HALF)]))
         return remote(staged.at[128:256], out.at[:, pl.ds(mine, HALF)], mate)
 
-    def partial(i, carry):
-        at = pl.ds(pl.multiple_of(i * 256, 256), 256)
-        total = nt(gkv[0, :, cols(0)], wv[0, 0, at, :])
-        for j in range(1, GROUPS):
-            total = total + nt(gkv[0, :, cols(j)], wv[0, j, at, :])
-        gxf[:, at] = total[0:128]
-        gxs[:, at] = total[128:256].astype(BF)
-        return carry
-
-    fz = [rise(i) for i in range(4)]
+    def partial():
+        for i in range(8):
+            at = pl.ds(i * 256, 256)
+            total = nt(gkv[0, :, cols(0)], wv[0, 0, at, :])
+            for j in range(1, GROUPS):
+                total = total + nt(gkv[0, :, cols(j)], wv[0, j, at, :])
+            gxf[:, at] = total[0:128]
+            gxs[:, at] = total[128:256].astype(BF)
+
+    fz = [rise(i) for i in range(8)]
     in_q.wait()
     in_g.wait()
     arrive([m_q, m_g])
     bz, bx = [], []
     for i in range(4):
         bz.append(attend(i, fz[i]))
-        fz.append(rise(4 + i))
     f1, a1 = forward(1)
     f3, a3 = forward(3)
     bz.append(attend(4, fz[4]))
+    bx.append(return_x(0, bz[0]))
     bz.append(attend(5, fz[5]))
-    bx.append(return_x(0, bz[0]))
     bx.append(return_x(1, bz[1]))
     bz.append(attend(6, fz[6]))
     bx.append(return_x(2, bz[2]))
     bz.append(attend(7, fz[7]))
     given = [give(ao, att_o), give(qo, gq_o)]
     bx.append(return_x(3, bz[3]))
+    finish(0, bx[0])
     bx.append(return_x(4, bz[4]))
-    finish(0, bx[0])
+    finish(1, bx[1])
     bx.append(return_x(5, bz[5]))
-    finish(1, bx[1])
+    finish(2, bx[2])
     bx.append(return_x(6, bz[6]))
-    finish(2, bx[2])
+    finish(3, bx[3])
+    gy0 = send_y(0)
     bx.append(return_x(7, bz[7]))
     arrive([a1, a3])
     f2 = remote(xa.at[512:640], xa.at[640:768], mate)
-    finish(3, bx[3])
     finish(4, bx[4])
     finish(5, bx[5])
-    gy0 = send_y(0)
     finish(6, bx[6])
+    gy1 = send_y(1)
     finish(7, bx[7])
-    gy1 = send_y(1)
+    gy2 = send_y(2)
     given.append(give(gkv.at[1], gv_o))
     arrive([m_x, f1, f3, f2])
     wa0 = weights(0, gy0)
     wa1 = weights(1, gy1)
+    wa2 = weights(2, gy2)
+    partial()
+    gxc = remote(gxs, gxr, mate)
     wb0 = second(0, wa0)
-    lax.fori_loop(0, 8, partial, 0)
-    gxc = remote(gxs, gxr, mate)
     wb1 = second(1, wa1)
+    wb2 = second(2, wa2)
     wc0 = third(0, wb0)
-    wc1 = third(1, wb1)
     arrive([gxc])
     gx_o[...] = (gxf[...] + gxr[...].astype(F32)).astype(BF)
+    wc1 = third(1, wb1)
+    wc2 = third(2, wb2)
     assemble(0, wc0)
     assemble(1, wc1)
+    assemble(2, wc2)
     arrive(given)
     assert count[0] <= SENDS and arrivals[0] <= LANDINGS, (count, arrivals)
     for copy in stored:

time: 66.8 us -> 61.7 us (0.924)
  Pallas kernels: 65.9 us -> 60.8 us
    pallas_call x1, Pallas kernels: 64.4 us -> 59.3 us  [body(): pl.pallas_call(kernel, out_shape=held, in_specs=[anywhere] * 6, out_specs...]
where the time goes in v3:
time: 61.7 us; the launch traced here: 61.6 us
  Pallas kernels  60.8 us (99%)
  between operations  0.8 us (1%)
    pallas_call x1, Pallas kernels, body(): pl.pallas_call(kernel, out_shape=held, in_specs=[anywhere] * 6, out_specs...  59.3 us
    pallas_call x1, Pallas kernels, body(): pl.pallas_call(hand_over, out_shape=shapes, in_specs=[pl.BlockSpec(memory...  1.53 us

profile of v3, /device:TPU:1, one launch (start us, length us, event | category | flops | bytes accessed | tf_op | source)
XLA Modules:
  0.0 61.6 jit_solution(16480807431379442641)
XLA Ops:
  0.6 59.3 %hierarchical_attention.1 = (bf16[128,2048]{1,0:T(8,128)(2,1)S(1)}, bf16[128,2048]{1,0:T(8,128)(2,1)S(1)}, bf16[128,2048]{1,0:T(8,128)(2,1)S(1)}, bf16[128,2048]{1,0:T(8,128)(2,1)S(1)}, f32[64,2048]{1,0:T(8,128)S(1)}) custom-call(bf16[128,2048]{1,0:T(8,128)(2,1)} %bitcast.8, bf16[128,2048]{1,0:T(8,128)(2,1)} %bitcast.9, bf16[128,2048]{1,0:T(8,128)(2,1)} %bitcast.10, ...), custom_call_target="tpu_custom_call" | custom-call | tf_op jit(solution)/shard_map/hierarchical_attention/pallas_call | solution.py:540
  59.9 1.5 %hand_over.1 = (bf16[128,2048]{1,0:T(8,128)(2,1)}, bf16[128,2048]{1,0:T(8,128)(2,1)}, bf16[128,2048]{1,0:T(8,128)(2,1)}, bf16[128,2048]{1,0:T(8,128)(2,1)}, f32[64,2048]{1,0:T(8,128)}) custom-call(bf16[128,2048]{1,0:T(8,128)(2,1)S(1)} %get-tuple-element.15.refs_0_, bf16[128,2048]{1,0:T(8,128)(2,1)S(1)} %get-tuple-element.16.refs_1_, ...), custom_call_target="tpu_custom_call" | custom-call | tf_op jit(solution)/shard_map/hand_over/pallas_call | solution.py:552

commit v4 on v3

--- a/solution.py
+++ b/solution.py
@@ -25,12 +25,12 @@
 
 
 def matrices():
-    pool = np.zeros((112, 384), np.float32)
+    pool = np.zeros((112, 432), np.float32)
     for tok in range(128):
         pool[tok // 2, tok] = 0.5
         pool[64 + tok // 4, tok] = 0.25
         pool[96 + tok // 8, tok] = 0.125
-    rise = np.zeros((96, 384), np.float32)
+    rise = np.zeros((96, 432), np.float32)
     for row in range(64):
         rise[row // 4, row] = 0.25
         rise[64 + row // 8, row] = 0.125
@@ -38,23 +38,21 @@
         rise[72 + row // 8, 128 + row] = 0.125
         rise[32 + row // 2, 192 + row] = 0.5
         rise[80 + row // 4, 192 + row] = 0.25
-    third = np.zeros((64, 128), np.float32)
+    third = np.zeros((64, 432), np.float32)
     for row in range(64):
         third[row, row] = 1.0
         third[row, 64 + row // 2] = 0.5
         third[row, 96 + row // 2] = 0.5
-    back = np.zeros((128, 384), np.float32)
-    for row in range(64):
-        back[row, :128] = third[16 + row // 4] * 0.25
-        back[64 + row, :128] = third[32 + row // 2] * 0.5
-    spread = np.zeros((256, 384), np.float32)
+    spread = np.zeros((256, 432), np.float32)
     for tok in range(256):
         spread[tok, tok // 2] = 0.5
         spread[tok, 128 + tok // 4] = 0.25
         spread[tok, 192 + tok // 8] = 0.125
         spread[tok, 224 + tok // 8] = 0.125
-        spread[tok, 256:384] = third[tok // 16] / 16
-    return np.concatenate([pool, rise, back, spread], 0)
+        for k in range(3):
+            spread[tok, 256 + 16 * k + tok // 16] = 1 / 16
+        spread[tok, 304:432] = third[tok // 16, :128] / 16
+    return np.concatenate([pool, rise, third, spread], 0)
 
 
 def flipped(place, k):
@@ -93,9 +91,8 @@
     sp=((2, 2, 48, HALF), BF),
     sz=((2, 96, HALF), BF),
     dcb=((2, 256, HALF), BF),
-    dcf=((2, 128, HALF), F32),
-    rb=((2, 384, HALF), BF),
-    sx=((2, 128, HALF), BF),
+    rb=((2, 432, HALF), BF),
+    sx=((2, 64, HALF), BF),
     ld=((2, 256, HALF), F32),
     gkv=((2, 256, HALF), BF),
     ao=((256, HALF), BF),
@@ -128,7 +125,7 @@
     gxf=((128, D), F32),
     gxs=((128, D), BF),
     gxr=((128, D), BF),
-    pp=((592, 384), BF),
+    pp=((528, 432), BF),
 )
 
 
@@ -136,7 +133,7 @@
     s = dict(zip(SCRATCH, rest[: len(SCRATCH)]))
     ssem, rsem = rest[len(SCRATCH) :]
     xa, wv, qv, gv, kl, vl, kt, vt, lo = (s[n] for n in ("xa", "wv", "qv", "gv", "kl", "vl", "kt", "vt", "lo"))
-    cc, sp, sz, dcb, dcf, rb, sx, ld = (s[n] for n in ("cc", "sp", "sz", "dcb", "dcf", "rb", "sx", "ld"))
+    cc, sp, sz, dcb, rb, sx, ld = (s[n] for n in ("cc", "sp", "sz", "dcb", "rb", "sx", "ld"))
     gkv, ao, qo, gs = (s[n] for n in ("gkv", "ao", "qo", "gs"))
     gt, rs, ra, tf, tb, rz, fo, ow = ([s[n + p] for p in "012"] for n in ("gt", "rs", "ra", "tf", "tb", "rz", "fo", "ow"))
     gxf, gxs, gxr, pp = (s[n] for n in ("gxf", "gxs", "gxr", "pp"))
@@ -167,6 +164,7 @@
 
     class Landing:
         def __init__(self, whole, send_at):
+            self.at = arrivals[0]
             self.copy = pltpu.make_async_remote_copy(
                 src_ref=whole,
                 dst_ref=whole,
@@ -189,9 +187,11 @@
             sent.append((total, self.at))
 
         def send(self, whole, messages):
-            landing = Landing(whole, self.at)
+            return self.add(Landing(whole, self.at), messages)
+
+        def add(self, landing, messages):
             for src, dst, device in messages:
-                start(src, dst, device, self.at, arrivals[0] - 1)
+                start(src, dst, device, self.at, landing.at)
             return landing
 
     def remote(src, dst, device):
@@ -250,7 +250,7 @@
 
     pl.semaphore_wait(barrier, len(peers))
     fx_route, fz_route = Route(cc.at[:, 0:128]), Route(cc.at[:, 128:256])
-    bx_route, bz_route = Route(rb.at[:, 128:256]), Route(rb.at[:, 256:384])
+    bx_route, bz_route = Route(rb.at[:, 128:304]), Route(rb.at[:, 304:432])
 
     def send_x(i):
         at = head_cols(i)
@@ -258,8 +258,8 @@
         for h, line in ((0, along_x), (1, cross_x)):
             first = sp.at[h, :, 0:32, at]
             second = sp.at[h, :, 32:48, at]
+            messages.append((second, cc.at[:, 64 + 16 * h : 80 + 16 * h, at], line[2]))
             messages.append((first, cc.at[:, 32 * h : 32 * h + 32, at], line[1]))
-            messages.append((second, cc.at[:, 64 + 16 * h : 80 + 16 * h, at], line[2]))
             messages.append((second, cc.at[:, 96 + 16 * h : 112 + 16 * h, at], line[3]))
         return fx_route.send(cc.at[:, 0:128, at], messages)
 
@@ -289,8 +289,8 @@
         return fz_route.send(
             cc.at[:, 128:256, at],
             [
+                (sz.at[:, 64:96, at], cc.at[:, 192:224, at], along_z[2]),
                 (sz.at[:, 0:64, at], cc.at[:, 128:192, at], along_z[1]),
-                (sz.at[:, 64:96, at], cc.at[:, 192:224, at], along_z[2]),
                 (sz.at[:, 64:96, at], cc.at[:, 224:256, at], along_z[3]),
             ],
         )
@@ -321,10 +321,8 @@
         qo[:, c] = dq.astype(BF)
         dck = tn(d1, q) * fold
         dcv = tn(p1b, g) * 0.25
-        dcf[0, :, c] = dck[0:128]
-        dcf[1, :, c] = dcv[0:128]
-        dcb[0, 128:256, c] = dck[128:256].astype(BF)
-        dcb[1, 128:256, c] = dcv[128:256].astype(BF)
+        dcb[0, :, c] = dck.astype(BF)
+        dcb[1, :, c] = dcv.astype(BF)
         for b in (0, 1):
             dk = tn(d0[b], q[pair[b]]) * fold
             dv = tn(p0b[b], g[pair[b]]) * 0.25
@@ -338,34 +336,39 @@
         arrive([landing])
         at = head_cols(i)
         head(at)
-        return bz_route.send(
-            rb.at[:, 256:384, at],
+        along = bz_route.send(
+            rb.at[:, 304:432, at],
             [
-                (dcb.at[:, 128:192, at], rb.at[:, 256:320, at], along_z[1]),
-                (dcb.at[:, 192:224, at], rb.at[:, 320:352, at], along_z[2]),
-                (dcb.at[:, 224:256, at], rb.at[:, 352:384, at], along_z[3]),
+                (dcb.at[:, 192:224, at], rb.at[:, 368:400, at], along_z[2]),
+                (dcb.at[:, 128:192, at], rb.at[:, 304:368, at], along_z[1]),
+                (dcb.at[:, 224:256, at], rb.at[:, 400:432, at], along_z[3]),
             ],
         )
-
-    def return_x(i, landing):
-        arrive([landing])
+        across = bx_route.send(
+            rb.at[:, 128:304, at],
+            [
+                (dcb.at[:, 64:96, at], rb.at[:, 192:224, at], along_x[2]),
+                (dcb.at[:, 0:64, at], rb.at[:, 128:192, at], along_x[1]),
+                (dcb.at[:, 96:128, at], rb.at[:, 224:256, at], along_x[3]),
+            ],
+        )
+        return along, across
+
+    def return_x(i, landings):
+        along, across = landings
+        arrive([along])
         at = head_cols(i)
         for kv in (0, 1):
-            sx[kv, :, at] = (dcf[kv, :, at] + nn(pp[208:336, 0:128], rb[kv, 256:384, at])).astype(BF)
-        return bx_route.send(
-            rb.at[:, 128:256, at],
-            [
-                (sx.at[:, 0:64, at], rb.at[:, 128:192, at], along_x[1]),
-                (sx.at[:, 64:96, at], rb.at[:, 192:224, at], along_x[2]),
-                (sx.at[:, 96:128, at], rb.at[:, 224:256, at], along_x[3]),
-            ],
+            sx[kv, :, at] = nn(pp[208:272, 0:128], rb[kv, 304:432, at]).astype(BF)
+        return bx_route.add(
+            across, [(sx.at[:, 16 * k : 16 * k + 16, at], rb.at[:, 240 + 16 * k : 256 + 16 * k, at], along_x[k]) for k in (2, 1, 3)]
         )
 
     def finish(i, landing):
         arrive([landing])
         at = head_cols(i)
         for kv in (0, 1):
-            total = ld[kv, :, at] + nn(pp[336:592, :], rb[kv, :, at])
+            total = ld[kv, :, at] + nn(pp[272:528, :], rb[kv, :, at])
             gkv[kv, :, at] = total.astype(BF)
             if kv == 0:
                 gs[at, :] = total.T.astype(BF)
@@ -376,7 +379,7 @@
         quarter = [pl.ds(pl.multiple_of(first * DH + flipped(y, k) * each, 32), each) for k in range(4)]
         landing = Route(gt[p].at[:, 256:1024]).send(
             gt[p].at[:, 256:1024],
-            [(gs.at[quarter[k]], gt[p].at[:, k * 256 : (k + 1) * 256], along_y[k]) for k in (1, 2, 3)],
+            [(gs.at[quarter[k]], gt[p].at[:, k * 256 : (k + 1) * 256], along_y[k]) for k in (2, 1, 3)],
         )
         gt[p][:, 0:256] = gs[quarter[0], :]
         return landing
@@ -460,23 +463,25 @@
             gxf[:, at] = total[0:128]
             gxs[:, at] = total[128:256].astype(BF)
 
-    fz = [rise(i) for i in range(8)]
+    fz = [rise(i) for i in range(7)]
     in_q.wait()
     in_g.wait()
     arrive([m_q, m_g])
     bz, bx = [], []
     for i in range(4):
         bz.append(attend(i, fz[i]))
+        if i < 1:
+            fz.append(rise(7 + i))
     f1, a1 = forward(1)
     f3, a3 = forward(3)
     bz.append(attend(4, fz[4]))
+    bz.append(attend(5, fz[5]))
     bx.append(return_x(0, bz[0]))
-    bz.append(attend(5, fz[5]))
+    bz.append(attend(6, fz[6]))
     bx.append(return_x(1, bz[1]))
-    bz.append(attend(6, fz[6]))
-    bx.append(return_x(2, bz[2]))
     bz.append(attend(7, fz[7]))
     given = [give(ao, att_o), give(qo, gq_o)]
+    bx.append(return_x(2, bz[2]))
     bx.append(return_x(3, bz[3]))
     finish(0, bx[0])
     bx.append(return_x(4, bz[4]))

time: 61.7 us -> 61.5 us (level)
  no operation moved by 1% of the time
where the time goes in v4:
time: 61.5 us; the launch traced here: 61.4 us
  Pallas kernels  60.6 us (99%)
  between operations  0.8 us (1%)
    pallas_call x1, Pallas kernels, body(): pl.pallas_call(kernel, out_shape=held, in_specs=[anywhere] * 6, out_specs...  59.1 us
    pallas_call x1, Pallas kernels, body(): pl.pallas_call(hand_over, out_shape=shapes, in_specs=[pl.BlockSpec(memory...  1.53 us

profile of v4, /device:TPU:1, one launch (start us, length us, event | category | flops | bytes accessed | tf_op | source)
XLA Modules:
  0.0 61.4 jit_solution(10482013438965640748)
XLA Ops:
  0.6 59.1 %hierarchical_attention.1 = (bf16[128,2048]{1,0:T(8,128)(2,1)S(1)}, bf16[128,2048]{1,0:T(8,128)(2,1)S(1)}, bf16[128,2048]{1,0:T(8,128)(2,1)S(1)}, bf16[128,2048]{1,0:T(8,128)(2,1)S(1)}, f32[64,2048]{1,0:T(8,128)S(1)}) custom-call(bf16[128,2048]{1,0:T(8,128)(2,1)} %bitcast.8, bf16[128,2048]{1,0:T(8,128)(2,1)} %bitcast.9, bf16[128,2048]{1,0:T(8,128)(2,1)} %bitcast.10, ...), custom_call_target="tpu_custom_call" | custom-call | tf_op jit(solution)/shard_map/hierarchical_attention/pallas_call | solution.py:545
  59.7 1.5 %hand_over.1 = (bf16[128,2048]{1,0:T(8,128)(2,1)}, bf16[128,2048]{1,0:T(8,128)(2,1)}, bf16[128,2048]{1,0:T(8,128)(2,1)}, bf16[128,2048]{1,0:T(8,128)(2,1)}, f32[64,2048]{1,0:T(8,128)}) custom-call(bf16[128,2048]{1,0:T(8,128)(2,1)S(1)} %get-tuple-element.15.refs_0_, bf16[128,2048]{1,0:T(8,128)(2,1)S(1)} %get-tuple-element.16.refs_1_, ...), custom_call_target="tpu_custom_call" | custom-call | tf_op jit(solution)/shard_map/hand_over/pallas_call | solution.py:557

commit v5 on v4

--- a/solution.py
+++ b/solution.py
@@ -295,7 +295,7 @@
             ],
         )
 
-    def head(c):
+    def head(c, send):
         q = qv[:, c]
         g = gv[:, c]
         ck = cc[0, :, c]
@@ -323,6 +323,7 @@
         dcv = tn(p1b, g) * 0.25
         dcb[0, :, c] = dck.astype(BF)
         dcb[1, :, c] = dcv.astype(BF)
+        landings = send()
         for b in (0, 1):
             dk = tn(d0[b], q[pair[b]]) * fold
             dv = tn(p0b[b], g[pair[b]]) * 0.25
@@ -331,28 +332,32 @@
             other = slice(64 - 64 * b, 128 - 64 * b)
             rb[0, other, c] = dk[128:192].astype(BF)
             rb[1, other, c] = dv[128:192].astype(BF)
+        return landings
 
     def attend(i, landing):
         arrive([landing])
         at = head_cols(i)
-        head(at)
-        along = bz_route.send(
-            rb.at[:, 304:432, at],
-            [
-                (dcb.at[:, 192:224, at], rb.at[:, 368:400, at], along_z[2]),
-                (dcb.at[:, 128:192, at], rb.at[:, 304:368, at], along_z[1]),
-                (dcb.at[:, 224:256, at], rb.at[:, 400:432, at], along_z[3]),
-            ],
-        )
-        across = bx_route.send(
-            rb.at[:, 128:304, at],
-            [
-                (dcb.at[:, 64:96, at], rb.at[:, 192:224, at], along_x[2]),
-                (dcb.at[:, 0:64, at], rb.at[:, 128:192, at], along_x[1]),
-                (dcb.at[:, 96:128, at], rb.at[:, 224:256, at], along_x[3]),
-            ],
-        )
-        return along, across
+
+        def send():
+            along = bz_route.send(
+                rb.at[:, 304:432, at],
+                [
+                    (dcb.at[:, 192:224, at], rb.at[:, 368:400, at], along_z[2]),
+                    (dcb.at[:, 128:192, at], rb.at[:, 304:368, at], along_z[1]),
+                    (dcb.at[:, 224:256, at], rb.at[:, 400:432, at], along_z[3]),
+                ],
+            )
+            across = bx_route.send(
+                rb.at[:, 128:304, at],
+                [
+                    (dcb.at[:, 64:96, at], rb.at[:, 192:224, at], along_x[2]),
+                    (dcb.at[:, 0:64, at], rb.at[:, 128:192, at], along_x[1]),
+                    (dcb.at[:, 96:128, at], rb.at[:, 224:256, at], along_x[3]),
+                ],
+            )
+            return along, across
+
+        return head(at, send)
 
     def return_x(i, landings):
         along, across = landings

time: 61.5 us -> 61.6 us (level)
  no operation moved by 1% of the time
where the time goes in v5:
time: 61.6 us; the launch traced here: 61.4 us
  Pallas kernels  60.6 us (98%)
  between operations  0.8 us (1%)
    pallas_call x1, Pallas kernels, body(): pl.pallas_call(kernel, out_shape=held, in_specs=[anywhere] * 6, out_specs...  59.1 us
    pallas_call x1, Pallas kernels, body(): pl.pallas_call(hand_over, out_shape=shapes, in_specs=[pl.BlockSpec(memory...  1.53 us

profile of v5, /device:TPU:1, one launch (start us, length us, event | category | flops | bytes accessed | tf_op | source)
XLA Modules:
  0.0 61.4 jit_solution(3268751011549162048)
XLA Ops:
  0.6 59.1 %hierarchical_attention.1 = (bf16[128,2048]{1,0:T(8,128)(2,1)S(1)}, bf16[128,2048]{1,0:T(8,128)(2,1)S(1)}, bf16[128,2048]{1,0:T(8,128)(2,1)S(1)}, bf16[128,2048]{1,0:T(8,128)(2,1)S(1)}, f32[64,2048]{1,0:T(8,128)S(1)}) custom-call(bf16[128,2048]{1,0:T(8,128)(2,1)} %bitcast.8, bf16[128,2048]{1,0:T(8,128)(2,1)} %bitcast.9, bf16[128,2048]{1,0:T(8,128)(2,1)} %bitcast.10, ...), custom_call_target="tpu_custom_call" | custom-call | tf_op jit(solution)/shard_map/hierarchical_attention/pallas_call | solution.py:550
  59.8 1.5 %hand_over.1 = (bf16[128,2048]{1,0:T(8,128)(2,1)}, bf16[128,2048]{1,0:T(8,128)(2,1)}, bf16[128,2048]{1,0:T(8,128)(2,1)}, bf16[128,2048]{1,0:T(8,128)(2,1)}, f32[64,2048]{1,0:T(8,128)}) custom-call(bf16[128,2048]{1,0:T(8,128)(2,1)S(1)} %get-tuple-element.15.refs_0_, bf16[128,2048]{1,0:T(8,128)(2,1)S(1)} %get-tuple-element.16.refs_1_, ...), custom_call_target="tpu_custom_call" | custom-call | tf_op jit(solution)/shard_map/hand_over/pallas_call | solution.py:562
